TPU v7x, 256 devices: a whole 4x4x8 slice. The times are simulated.
256 devices in a mesh: store: 32 (over x, z), tensor: 8 (over y, core).
Axes of the slice: x: 4, y: 4, z: 8, core: 2. Of those that a mesh axis runs over, the one named last changes fastest.
Arguments:
- hidden: bfloat16 [32768, 12288], P('store', 'tensor'), may hold values from -6 to 6
- kv_weight: bfloat16 [12288, 2048], P('tensor', 'store'), may hold values from -0.0546875 to 0.0546875
- pages: bfloat16 [1024, 128, 2048], P('store', None, 'tensor'), may hold values from -8 to 8
- queries: bfloat16 [32768, 6144], P('store', 'tensor'), may hold values from -8 to 8
- page_owner: int32 [64, 16], replicated, may hold values from 0 to 31, as said below
- page_slot: int32 [64, 16], replicated, may hold values from 0 to 31
- span_order: int32 [64, 16], P('store'), may hold values from 0 to 15, each once within a row
- positions: int32 [64, 16, 32], P('store'), may hold values from 2 to 127, as said below
- counts: int32 [64, 16], P('store'), may hold values from 1 to 32, as said below
Outputs:
- attended: bfloat16 [32768, 6144], P('store', 'tensor')
- new_kv: bfloat16 [32768, 2048], P('store', 'tensor')
Inputs may be any that keep to these rules, and one draw needn't show every extreme that they name: `page_owner`: request r is served at store index r // 2. Among the 32 pages of the requests served at one store index, each owner holds at most 2, and some owner exactly 2. `positions`: each row increases strictly. `counts`: every request has a span with 32.
All inputs are finite; a program needn't handle non-finite values.
Results may differ from a plain program's by a relative error of at most 0.0053.
Values may be sent and summed in bfloat16 or wider, within the bound.
No kernel may reach another device: no remote copies, remote signals or barrier semaphores. Data moves between devices by JAX's collectives and lax.ppermute only.
A program may use at most 128 MiB of HBM per device.

v0:
```python
import jax
import jax.numpy as jnp
from jax import lax
from jax.sharding import PartitionSpec as P

HEAD = 128


def blend_attend(request_queries, fresh_rows, cached, span_rank, recompute_pos, row_used):
    spans, span_len, kv_width = cached.shape
    per_span = recompute_pos.shape[1]
    kv_heads = kv_width // (2 * HEAD)
    head_group = request_queries.shape[1] // (kv_heads * HEAD)
    marked = (recompute_pos[:, :, None] == jnp.arange(span_len)[None, None, :]) & row_used[
        :, :, None
    ]
    placed = jnp.einsum(
        "cjt,cjw->ctw",
        marked.astype(jnp.bfloat16),
        fresh_rows.reshape(spans, per_span, kv_width),
        preferred_element_type=jnp.float32,
    )
    replaced = jnp.any(marked, axis=1)[:, :, None]
    blended = jnp.where(replaced, placed.astype(jnp.bfloat16), cached)
    key_value = blended.reshape(spans * span_len, kv_heads, 2, HEAD)
    query_rows = request_queries.reshape(spans * per_span, kv_heads, head_group, HEAD)
    scores = jnp.einsum(
        "qhgd,khd->hgqk", query_rows, key_value[:, :, 0], preferred_element_type=jnp.float32
    ) * HEAD ** (-0.5)
    query_span = jnp.arange(spans * per_span) // per_span
    key_span = jnp.arange(spans * span_len) // span_len
    key_place = jnp.arange(spans * span_len) % span_len
    query_place = recompute_pos.reshape(-1)
    query_rank = jnp.repeat(span_rank, per_span)
    key_rank = jnp.repeat(span_rank, span_len)
    earlier = key_rank[None, :] < query_rank[:, None]
    causal = (key_span[None, :] == query_span[:, None]) & (
        key_place[None, :] <= query_place[:, None]
    )
    allowed = earlier | causal
    scores = jnp.where(allowed[None, None], scores, -1e30)
    peak = jnp.max(scores, axis=-1, keepdims=True)
    raised = jnp.exp(scores - peak)
    weights = (raised / jnp.sum(raised, axis=-1, keepdims=True)).astype(jnp.bfloat16)
    mixed = jnp.einsum(
        "hgqk,khd->qhgd", weights, key_value[:, :, 1], preferred_element_type=jnp.float32
    )
    mixed = mixed.reshape(spans * per_span, -1) * row_used.reshape(-1, 1).astype(jnp.float32)
    return mixed.astype(jnp.bfloat16)


def body(hidden, kv_weight, pages, queries, page_owner, page_slot, span_order, positions, counts):
    store_count = lax.axis_size("store")
    store_index = lax.axis_index("store")
    req_local, spans = span_order.shape
    per_span = positions.shape[2]
    entries = req_local * spans
    slot_depth = max(2, 2 * entries // store_count)
    span_len = pages.shape[1]
    kv_width = pages.shape[2]
    partial_kv = jnp.dot(
        hidden,
        lax.all_gather(kv_weight, "store", axis=1, tiled=True),
        preferred_element_type=jnp.float32,
    )
    summed = lax.psum(partial_kv, "tensor")
    own_kv = lax.dynamic_slice_in_dim(summed, lax.axis_index("tensor") * kv_width, kv_width, 1)
    row_used = jnp.arange(per_span)[None, None, :] < counts[:, :, None]
    new_kv = (own_kv * row_used.reshape(-1, 1).astype(jnp.float32)).astype(jnp.bfloat16)
    owners = page_owner.reshape(store_count, entries)
    slot_table = page_slot.reshape(store_count, entries)
    before = jnp.arange(entries)[None, :] < jnp.arange(entries)[:, None]
    same_owner = owners[:, :, None] == owners[:, None, :]
    owner_rank = jnp.sum(same_owner & before[None], axis=2)
    picked = (owners == store_index)[:, :, None] & (
        owner_rank[:, :, None] == jnp.arange(slot_depth)[None, None, :]
    )
    source_slot = jnp.sum(picked * slot_table[:, :, None], axis=1)
    filled = jnp.any(picked, axis=1)
    outgoing = jnp.take(pages, source_slot.reshape(-1), axis=0)
    outgoing = jnp.where(filled.reshape(-1, 1, 1), outgoing, jnp.zeros((), jnp.bfloat16))
    outgoing = outgoing.reshape(store_count, slot_depth, span_len, kv_width)
    arrived = lax.all_to_all(outgoing, "store", split_axis=0, concat_axis=0, tiled=True)
    my_owner = lax.dynamic_index_in_dim(owners, store_index, 0, keepdims=False)
    my_rank = lax.dynamic_index_in_dim(owner_rank, store_index, 0, keepdims=False)
    flat_index = my_owner * slot_depth + my_rank
    cached = jnp.take(
        arrived.reshape(store_count * slot_depth, span_len, kv_width), flat_index, axis=0
    )
    cached = cached.reshape(req_local, spans, span_len, kv_width)
    query_request = queries.reshape(req_local, spans * per_span, queries.shape[1])
    fresh_request = new_kv.reshape(req_local, spans * per_span, kv_width)

    def one_request(inputs):
        return blend_attend(*inputs)

    attended = lax.map(
        one_request, (query_request, fresh_request, cached, span_order, positions, row_used)
    )
    return (attended.reshape(queries.shape), new_kv)


def solution(mesh):
    placed = (
        P("store", "tensor"),
        P("tensor", "store"),
        P("store", None, "tensor"),
        P("store", "tensor"),
        P(),
        P(),
        P("store", None),
        P("store", None, None),
        P("store", None),
    )
    return jax.shard_map(
        body,
        mesh=mesh,
        in_specs=placed,
        out_specs=(P("store", "tensor"), P("store", "tensor")),
        check_vma=False,
    )
```

profile of v0, /device:TPU:1, one launch (start us, length us, event | category | flops | bytes accessed | tf_op | source)
XLA Modules:
  0.0 389.8 jit_solution(14286531549056555274)
XLA Ops:
  7.2 0.7 all-gather.2.cloned.1.call-update
  7.9 1.0 copy.34
  9.0 0.8 convert_reduce_fusion
  10.0 0.8 copy.36
  11.3 4.3 %gather_fusion = bf16[64,128,256]{2,1,0:T(8,128)(2,1)} fusion(bf16[32,128,256]{2,1,0:T(8,128)(2,1)} %param.13, s32[1024]{0:T(1024)S(1)} %pad_clamp_fusion.1), kind=kCustom, calls=%fused_computation | custom fusion | bytes 8388864 | tf_op jit(solution)/shard_map/jit(_take)/gather | solution.py:80
  15.7 3.9 select_select_fusion
  19.5 12.0 %all-to-all-start = ((bf16[32,2,128,256]{3,2,1,0:T(8,128)(2,1)}), bf16[32,2,128,256]{3,2,1,0:T(8,128)(2,1)}, u32[]{:S(2)}, u32[]{:S(2)}) async-start(bf16[32,2,128,256]{3,2,1,0:T(8,128)(2,1)} %select_select_fusion), calls=%async_computation | async-start | bytes 8388608 | tf_op jit(solution)/shard_map/all_to_all | solution.py:83
  31.6 130.1 %all-gather.2.cloned.1.call-done = bf16[1536,2048]{0,1:T(8,128)(2,1)} async-done(((bf16[1536,64]{0,1:T(8,128)(2,1)}), bf16[1536,2048]{0,1:T(8,128)(2,1)}) %all-gather.2.cloned.1.call-update) | async-done | bytes 6291472 | tf_op jit(solution)/shard_map/all_gather | solution.py:63
  161.6 10.7 %fusion.36 = f32[1024,2048]{1,0:T(8,128)} fusion(bf16[1024,1536]{1,0:T(8,128)(2,1)S(1)} %copy-done, bf16[1536,2048]{0,1:T(8,128)(2,1)} %all-gather.2.cloned.1.call-done), kind=kOutput, calls=%fused_computation.79 | convolution fusion | flops 6442450944 | bytes 17825792 | tf_op jit(solution)/shard_map/dot_general | solution.py:61
  172.4 0.6 copy-done.4
  173.2 0.5 broadcast.363
  173.7 0.7 fusion.33
  174.5 2.9 gather_fusion.1
  177.4 1.6 broadcast_select_fusion
  179.1 100.7 %all-reduce.2.cloned.1.call-done = f32[1024,2048]{1,0:T(8,128)} async-done(((f32[1024,2048]{1,0:T(8,128)}), f32[1024,2048]{1,0:T(8,128)}) %all-reduce.2.cloned.1.call-update) | async-done | bytes 8388624 | tf_op jit(solution)/shard_map/psum | solution.py:66
  279.8 2.2 multiply_convert_fusion
  282.0 99.1 %while.13 = (s32[]{:T(128)}, bf16[2,512,768]{2,1,0:T(8,128)(2,1)}, s32[2,16,32]{2,1,0:T(8,128)S(1)}, pred[2,16,32]{2,1,0:T(8,128)(4,1)S(1)}, bf16[2,512,256]{2,1...) while((s32[]{:T(128)}, bf16[2,512,768]{2,1,0:T(8,128)(2,1)}, ...), condition=%wide.region_8.9_spmd, body=%wide.region_4.8_spmd.sunk | while | flops 3337703936 | bytes 102130080 | solution.py:97
  282.4 0.2 fusion.65
  282.7 1.0 constant_dynamic-slice_fusion.11
  283.7 2.0 fusion.66
  285.7 0.3 reshape.466
  286.0 1.2 constant_dynamic-slice_fusion.10
  287.2 0.3 copy.57
  287.4 2.0 and_or_fusion.2
  289.5 2.5 fusion.67
  291.9 3.5 copy.58
  295.5 11.6 %fusion.68 = (f32[6,512]{1,0:T(8,128)S(1)}, f32[2048,512,6]{1,0,2:T(8,128)}) fusion(pred[512,2048]{0,1:T(8,128)(4,1)S(1)} %and_or_fusion.2, bf16[512,6,128]{0,2,1:T(8,128)(2,1)S(1)} %bitcast.94, bf16[2048,1,1,128]{3,2,0,1:T(2,128)(2,1)} %get-tuple-element.242), kind=kOutput, calls=%fused_computation.6.clone.1 | convolution fusion | flops 1629484032 | bytes 27537408 | tf_op jit(solution)/shard_map/while/body/eval_jaxpr/qhgd,khd->hgqk/dot_general | solution.py:27
  307.1 11.2 %fusion.69 = f32[6,512]{1,0:T(8,128)S(1)} fusion(f32[2048,512,6]{1,0,2:T(8,128)} %get-tuple-element.243, f32[6,512]{1,0:T(8,128)S(1)} %get-tuple-element.244, pred[512,2048]{0,1:T(8,128)(4,1)S(1)} %and_or_fusion.2), kind=kLoop, calls=%fused_computation.5.clone.1 | loop fusion | flops 25162752 | bytes 26238976 | tf_op jit(solution)/shard_map/while/body/eval_jaxpr/reduce_sum | solution.py:44
  318.3 11.8 %fusion.70 = f32[128,6,512]{2,0,1:T(8,128)S(1)} fusion(f32[2048,512,6]{1,0,2:T(8,128)} %get-tuple-element.243, f32[6,512]{1,0:T(8,128)S(1)} %fusion.69, f32[6,512]{1,0:T(8,128)S(1)} %get-tuple-element.244, pred[512,2048]{0,1:T(8,128)(4,1)S(1)} %and_or_fusion.2, bf16[2048,1,1,128]{0,3,2,1:T(8,128)(2,1)S(1)} %copy-done.2), kind=kOutput, calls=%fused_computation.7.clone.1 | convolution fusion | flops 1642070016 | bytes 28336128 | tf_op jit(solution)/shard_map/while/body/eval_jaxpr/hgqk,khd->qhgd/dot_general | solution.py:45
  330.1 0.2 fusion.71
  330.3 0.3 copy.59
  330.6 0.9 constant_dynamic-update-slice_fusion.2
  332.0 0.2 fusion.65
  332.2 1.0 constant_dynamic-slice_fusion.11
  333.2 2.0 fusion.66
  335.2 0.3 reshape.466
  335.5 1.2 constant_dynamic-slice_fusion.10
  336.7 0.3 copy.57
  337.0 2.0 and_or_fusion.2
  339.0 2.5 fusion.67
  341.5 3.5 copy.58
  345.0 11.6 %fusion.68 = (f32[6,512]{1,0:T(8,128)S(1)}, f32[2048,512,6]{1,0,2:T(8,128)}) fusion(pred[512,2048]{0,1:T(8,128)(4,1)S(1)} %and_or_fusion.2, bf16[512,6,128]{0,2,1:T(8,128)(2,1)S(1)} %bitcast.94, bf16[2048,1,1,128]{3,2,0,1:T(2,128)(2,1)} %get-tuple-element.242), kind=kOutput, calls=%fused_computation.6.clone.1 | convolution fusion | flops 1629484032 | bytes 27537408 | tf_op jit(solution)/shard_map/while/body/eval_jaxpr/qhgd,khd->hgqk/dot_general | solution.py:27
  356.6 11.2 %fusion.69 = f32[6,512]{1,0:T(8,128)S(1)} fusion(f32[2048,512,6]{1,0,2:T(8,128)} %get-tuple-element.243, f32[6,512]{1,0:T(8,128)S(1)} %get-tuple-element.244, pred[512,2048]{0,1:T(8,128)(4,1)S(1)} %and_or_fusion.2), kind=kLoop, calls=%fused_computation.5.clone.1 | loop fusion | flops 25162752 | bytes 26238976 | tf_op jit(solution)/shard_map/while/body/eval_jaxpr/reduce_sum | solution.py:44
  367.9 11.8 %fusion.70 = f32[128,6,512]{2,0,1:T(8,128)S(1)} fusion(f32[2048,512,6]{1,0,2:T(8,128)} %get-tuple-element.243, f32[6,512]{1,0:T(8,128)S(1)} %fusion.69, f32[6,512]{1,0:T(8,128)S(1)} %get-tuple-element.244, pred[512,2048]{0,1:T(8,128)(4,1)S(1)} %and_or_fusion.2, bf16[2048,1,1,128]{0,3,2,1:T(8,128)(2,1)S(1)} %copy-done.2), kind=kOutput, calls=%fused_computation.7.clone.1 | convolution fusion | flops 1642070016 | bytes 28336128 | tf_op jit(solution)/shard_map/while/body/eval_jaxpr/hgqk,khd->qhgd/dot_general | solution.py:45
  379.7 0.2 fusion.71
  379.9 0.3 copy.59
  380.1 0.9 constant_dynamic-update-slice_fusion.2
  381.1 1.9 copy-done.1
  (58 shorter events, 2.0 us)
Async XLA Ops:
  7.2 154.5 %copy-start = (bf16[1024,1536]{1,0:T(8,128)(2,1)S(1)}, bf16[1024,1536]{1,0:T(8,128)(2,1)}, u32[]{:S(2)}) copy-start(bf16[1024,1536]{1,0:T(8,128)(2,1)} %param.11) | copy-start | bytes 9437188
  7.2 154.4 %all-gather.2.cloned.1.call-start = ((), (), s32[]{:S(2)}) async-start(), calls=%async_computation.1 | async-start | bytes 6488064 | tf_op jit(solution)/shard_map/all_gather | solution.py:63
  19.5 155.0 %all-to-all-start = ((bf16[32,2,128,256]{3,2,1,0:T(8,128)(2,1)}), bf16[32,2,128,256]{3,2,1,0:T(8,128)(2,1)}, u32[]{:S(2)}, u32[]{:S(2)}) async-start(bf16[32,2,128,256]{3,2,1,0:T(8,128)(2,1)} %select_select_fusion), calls=%async_computation | async-start | bytes 8388608 | tf_op jit(solution)/shard_map/all_to_all | solution.py:83
  31.5 248.3 %all-reduce.2.cloned.1.call-start = ((), (), s32[]{:S(2)}) async-start(), calls=%async_computation.2 | async-start | bytes 16777216 | tf_op jit(solution)/shard_map/psum | solution.py:66
  172.4 0.7 copy-start.4
  174.5 107.5 %copy-start.3 = (s32[2,16,32]{2,1,0:T(8,128)S(1)}, s32[2,16,32]{2,1,0:T(8,128)}, u32[]{:S(2)}) copy-start(s32[2,16,32]{2,1,0:T(8,128)} %param.18) | copy-start | bytes 12292
  174.5 107.5 %copy-start.5 = (s32[2,16]{1,0:T(2,128)S(1)}, s32[2,16]{1,0:T(2,128)}, u32[]{:S(2)}) copy-start(s32[2,16]{1,0:T(2,128)} %param.17) | copy-start | bytes 388
  307.1 11.3 %copy-start.2 = (bf16[2048,1,1,128]{0,3,2,1:T(8,128)(2,1)S(1)}, bf16[2048,1,1,128]{0,3,2,1:T(8,128)(2,1)}, u32[]{:S(2)}) copy-start(bf16[2048,1,1,128]{0,3,2,1:T(8,128)(2,1)} %copy.58) | copy-start | bytes 1572868 | tf_op jit(solution)/shard_map/while
  356.6 11.3 %copy-start.2 = (bf16[2048,1,1,128]{0,3,2,1:T(8,128)(2,1)S(1)}, bf16[2048,1,1,128]{0,3,2,1:T(8,128)(2,1)}, u32[]{:S(2)}) copy-start(bf16[2048,1,1,128]{0,3,2,1:T(8,128)(2,1)} %copy.58) | copy-start | bytes 1572868 | tf_op jit(solution)/shard_map/while
  381.1 1.9 copy-start.1
Sparse Core Ops, SparseCore 0:
  10.6 150.9 all-gather.1
  172.5 107.2 all-reduce.1
where the time goes:
time: 391 us; the launch traced here: 390 us
  waiting for transfers between devices  231 us (59%)
  matrix products  61.5 us (16%)
  other arithmetic  36.9 us (9%)
  local copies, waits for them, and re-layouts  33.5 us (9%)
  between operations  14.2 us (4%)
  starting transfers between devices  12.1 us (3%)
    all_gather x1, waiting for transfers between devices, body(): lax.all_gather(kv_weight, 'store', axis=1, tiled=True)  130 us
    psum x1, waiting for transfers between devices, body(): summed = lax.psum(partial_kv, 'tensor')  101 us
    dot_general x2, matrix products, blend_attend(): jnp.einsum('hgqk,khd->qhgd', weights, key_value[:, :, 1], preferred_eleme...  23.6 us
    dot_general x2, matrix products, blend_attend(): jnp.einsum('qhgd,khd->hgqk', query_rows, key_value[:, :, 0], preferred_el...  23.2 us
    reduce_sum x2, other arithmetic, blend_attend(): jnp.sum(raised, axis=-1, keepdims=True)  22.5 us
    all_to_all x1, starting transfers between devices, body(): lax.all_to_all(outgoing, 'store', split_axis=0, concat_axis=0, tiled=True)  12 us
    dot_general x1, matrix products, body(): jnp.dot(hidden, lax.all_gather(kv_weight, 'store', axis=1, tiled=True), p...  10.7 us
  transfers between devices with their start and end apart: 3, of which 2 were waited for; matrix products, arithmetic and copies ran while one was open for 7% of the time, Pallas kernels for 0%

commit v1 on v0

v1 whole, which is shorter than its diff:
```python
import functools

import jax
import jax.numpy as jnp
from jax import lax
from jax.experimental import pallas as pl
from jax.experimental.pallas import tpu as pltpu
from jax.sharding import Mesh
from jax.sharding import PartitionSpec as P

HEAD = 128
BF16 = jnp.bfloat16
F32 = jnp.float32
STORE = ("x", "z")
TENSOR = ("y", "core")
NEG = -1e30
EXP2_SCALE = 1.4426950408889634 * HEAD**-0.5


def pack_kernel(slot_ref, pages_ref, out_ref, sems):
    count = out_ref.shape[0]

    def copy(i):
        return pltpu.make_async_copy(pages_ref.at[slot_ref[i]], out_ref.at[i], sems.at[i])

    def start(i, carry):
        copy(i).start()
        return carry

    def wait(i, carry):
        copy(i).wait()
        return carry

    lax.fori_loop(0, count, start, 0)
    lax.fori_loop(0, count, wait, 0)


def pack_pages(source_slot, pages):
    count = source_slot.shape[0]
    return pl.pallas_call(
        pack_kernel,
        out_shape=jax.ShapeDtypeStruct((count,) + pages.shape[1:], pages.dtype),
        in_specs=[
            pl.BlockSpec(memory_space=pltpu.SMEM),
            pl.BlockSpec(memory_space=pl.ANY),
        ],
        out_specs=pl.BlockSpec(memory_space=pl.ANY),
        scratch_shapes=[pltpu.SemaphoreType.DMA((count,))],
        cost_estimate=pl.CostEstimate(
            flops=0, bytes_accessed=4 * count * pages.shape[1] * pages.shape[2], transcendentals=0
        ),
    )(source_slot, pages)


def project_kernel(hidden_ref, weight_ref, out_ref):
    out_ref[0] = lax.dot_general(
        hidden_ref[...], weight_ref[...], (((1,), (1,)), ((), ())), preferred_element_type=F32
    ).astype(out_ref.dtype)


def project(hidden, weight_t, block):
    rows, width = hidden.shape
    columns = weight_t.shape[0]
    return pl.pallas_call(
        project_kernel,
        grid=(columns // block,),
        out_shape=jax.ShapeDtypeStruct((columns // block, rows, block), BF16),
        in_specs=[
            pl.BlockSpec((rows, width), lambda i: (0, 0)),
            pl.BlockSpec((block, width), lambda i: (i, 0)),
        ],
        out_specs=pl.BlockSpec((1, rows, block), lambda i: (i, 0, 0)),
        compiler_params=pltpu.CompilerParams(vmem_limit_bytes=40 << 20),
        cost_estimate=pl.CostEstimate(
            flops=2 * rows * width * columns,
            bytes_accessed=2 * (rows * width + columns * width + rows * columns),
            transcendentals=0,
        ),
    )(hidden, weight_t)


def attend_kernel(
    spans,
    per_span,
    page_ref,
    span_ref,
    count_ref,
    q_ref,
    new_ref,
    pos_row_ref,
    pos_lane_ref,
    arrived_ref,
    out_ref,
    raw,
    keys,
    values,
    scores,
    weights,
    sems,
):
    requests = raw.shape[0]
    span_len = arrived_ref.shape[1]
    heads = q_ref.shape[1] // HEAD
    half = heads * per_span
    rows_request = spans * per_span

    def copy(r, k):
        return pltpu.make_async_copy(
            arrived_ref.at[page_ref[r, k]],
            raw.at[r, pl.ds(k * span_len, span_len)],
            sems.at[r, k],
        )

    for r in range(requests):
        for k in range(spans):
            copy(r, k).start()
    values[:, :, HEAD:] = jnp.ones((requests, spans * span_len, HEAD), BF16)
    place = lax.broadcasted_iota(jnp.int32, (span_len, per_span), 0)
    slot = lax.broadcasted_iota(jnp.int32, (span_len, per_span), 1)
    lane = lax.broadcasted_iota(jnp.int32, (per_span, span_len), 1)
    sub = lax.broadcasted_iota(jnp.int32, (per_span, HEAD), 0)
    groups = [(r, g) for r in range(requests) for g in range(spans // 2)]

    def blend(r, k):
        c = span_ref[r, k]
        copy(r, k).wait()
        pos = pos_row_ref[pl.ds(r * spans + c, 1), :]
        marked = (place == pos) & (slot < count_ref[r, c])
        first = pl.multiple_of(r * rows_request + c * per_span, per_span)
        fresh = new_ref[pl.ds(first, per_span), :]
        placed = jnp.dot(marked.astype(F32).astype(BF16), fresh, preferred_element_type=F32)
        replaced = jnp.max(marked.astype(F32), axis=1, keepdims=True) > 0.5
        at = slice(k * span_len, (k + 1) * span_len)
        mixed = jnp.where(replaced, placed, raw[r, at, :].astype(F32)).astype(BF16)
        keys[r, at, :] = mixed[:, :HEAD]
        values[r, at, :HEAD] = mixed[:, HEAD:]

    def first_row(r, k):
        return pl.multiple_of(r * rows_request + span_ref[r, k] * per_span, per_span)

    def score(step):
        r, g = groups[step]
        length = (g + 1) * 2 * span_len
        stacked = []
        for k in (2 * g, 2 * g + 1):
            blend(r, k)
            block = q_ref[pl.ds(first_row(r, k), per_span), :]
            stacked += [block[:, h * HEAD : (h + 1) * HEAD] for h in range(heads)]
        scores[step % 2, :, :length] = lax.dot_general(
            jnp.concatenate(stacked, axis=0),
            keys[r, :length, :],
            (((1,), (1,)), ((), ())),
            preferred_element_type=F32,
        )

    def attend(step):
        r, g = groups[step]
        slot_now = step % 2
        length = (g + 1) * 2 * span_len
        for part, k in enumerate((2 * g, 2 * g + 1)):
            rows = slice(part * half, (part + 1) * half)
            own = k * span_len
            allowed = lane <= pos_lane_ref[pl.ds(first_row(r, k), per_span), :]
            allowed = jnp.concatenate([allowed] * heads, axis=0)
            diagonal = jnp.where(allowed, scores[slot_now, rows, own : own + span_len], NEG)
            peak = jnp.max(diagonal, axis=1, keepdims=True)
            if k:
                before = scores[slot_now, rows, :own]
                peak = jnp.maximum(peak, jnp.max(before, axis=1, keepdims=True))
                weights[slot_now, rows, :own] = jnp.exp2((before - peak) * EXP2_SCALE).astype(BF16)
            weights[slot_now, rows, own : own + span_len] = jnp.exp2(
                (diagonal - peak) * EXP2_SCALE
            ).astype(BF16)
            if own + span_len < length:
                weights[slot_now, rows, own + span_len : length] = jnp.zeros(
                    (half, length - own - span_len), BF16
                )
        mixed = jnp.dot(
            weights[slot_now, :, :length], values[r, :length, :], preferred_element_type=F32
        )
        mixed = mixed[:, :HEAD] / mixed[:, HEAD:]
        for part, k in enumerate((2 * g, 2 * g + 1)):
            used = sub < count_ref[r, span_ref[r, k]]
            for h in range(heads):
                at = part * half + h * per_span
                out_ref[pl.ds(first_row(r, k), per_span), h * HEAD : (h + 1) * HEAD] = jnp.where(
                    used, mixed[at : at + per_span], 0.0
                ).astype(BF16)

    score(0)
    for step in range(len(groups)):
        if step + 1 < len(groups):
            score(step + 1)
        attend(step)


def attend(page_at, span_at, counts, queries, new_kv, positions, arrived):
    requests, spans = span_at.shape
    per_span = positions.shape[2]
    span_len = arrived.shape[1]
    kv_width = arrived.shape[2]
    heads = queries.shape[1] // HEAD
    length = spans * span_len
    pos_row = positions.reshape(requests * spans, per_span)
    pos_lane = jnp.broadcast_to(
        positions.reshape(requests * spans * per_span, 1), (requests * spans * per_span, span_len)
    )
    smem = pl.BlockSpec(memory_space=pltpu.SMEM)
    vmem = pl.BlockSpec(memory_space=pltpu.VMEM)
    pair = 2 * heads * per_span
    return pl.pallas_call(
        functools.partial(attend_kernel, spans, per_span),
        out_shape=jax.ShapeDtypeStruct(queries.shape, BF16),
        in_specs=[smem, smem, smem, vmem, vmem, vmem, vmem, pl.BlockSpec(memory_space=pl.ANY)],
        out_specs=vmem,
        scratch_shapes=[
            pltpu.VMEM((requests, length, kv_width), BF16),
            pltpu.VMEM((requests, length, HEAD), BF16),
            pltpu.VMEM((requests, length, 2 * HEAD), BF16),
            pltpu.VMEM((2, pair, length), F32),
            pltpu.VMEM((2, pair, length), BF16),
            pltpu.SemaphoreType.DMA((requests, spans)),
        ],
        compiler_params=pltpu.CompilerParams(vmem_limit_bytes=48 << 20),
        cost_estimate=pl.CostEstimate(
            flops=2 * requests * pair * length * HEAD * 3 * spans // 4,
            bytes_accessed=4 * queries.size + 2 * arrived.size,
            transcendentals=requests * pair * length * spans // 4,
        ),
    )(page_at, span_at, counts, queries, new_kv, pos_row, pos_lane, arrived)


def gather_weight(weight_t):
    return lax.all_gather(weight_t, STORE, axis=0, tiled=True)


def body(hidden, kv_weight, pages, queries, page_owner, page_slot, span_order, positions, counts):
    stores = lax.axis_size(STORE)
    tensors = lax.axis_size(TENSOR)
    store_index = lax.axis_index(STORE)
    requests, spans = span_order.shape
    per_span = positions.shape[2]
    entries = requests * spans
    span_len, kv_width = pages.shape[1:]

    owners = page_owner.reshape(stores, entries)
    slots = page_slot.reshape(stores, entries)
    entry = jnp.arange(entries)[None, :]
    mine = owners == store_index
    code = entry * pages.shape[0] + slots
    first = jnp.min(jnp.where(mine, code, entries * pages.shape[0]), axis=1)
    last = jnp.max(jnp.where(mine, code, 0), axis=1)
    source_slot = jnp.stack([first, last], axis=1).reshape(-1) % pages.shape[0]
    outgoing = pack_pages(source_slot, pages).reshape(stores, 2, span_len, kv_width)
    arrived = lax.all_to_all(outgoing, STORE, split_axis=0, concat_axis=0, tiled=True)
    arrived = arrived.reshape(stores * 2, span_len, kv_width)

    weight_t = gather_weight(kv_weight.T)
    partial_kv = project(hidden, weight_t, kv_width)
    own_kv = lax.psum_scatter(partial_kv, TENSOR, scatter_dimension=0, tiled=True)
    own_kv = own_kv.reshape(entries * per_span, kv_width)
    row_used = jnp.arange(per_span)[None, None, :] < counts[:, :, None]
    new_kv = jnp.where(row_used.reshape(-1, 1), own_kv, jnp.zeros((), BF16))

    my_owner = lax.dynamic_index_in_dim(owners, store_index, 0, keepdims=False)
    earlier = jnp.arange(entries)[None, :] < jnp.arange(entries)[:, None]
    second = jnp.any((my_owner[:, None] == my_owner[None, :]) & earlier, axis=1)
    page_of = (my_owner * 2 + second.astype(jnp.int32)).reshape(requests, spans)
    at_rank = span_order[:, None, :] == jnp.arange(spans)[None, :, None]
    span_at = jnp.sum(at_rank * jnp.arange(spans)[None, None, :], axis=2)
    page_at = jnp.sum(at_rank * page_of[:, None, :], axis=2)
    attended = attend(page_at, span_at, counts, queries, new_kv, positions, arrived)
    return attended, new_kv


def solution(mesh):
    split = Mesh(mesh.devices.reshape(4, 8, 4, 2), STORE + TENSOR)
    return jax.shard_map(
        body,
        mesh=split,
        in_specs=(
            P(STORE, TENSOR),
            P(TENSOR, STORE),
            P(STORE, None, TENSOR),
            P(STORE, TENSOR),
            P(),
            P(),
            P(STORE, None),
            P(STORE, None, None),
            P(STORE, None),
        ),
        out_specs=(P(STORE, TENSOR), P(STORE, TENSOR)),
        check_vma=False,
    )
```

time: 391 us -> 378 us (0.967)
  Pallas kernels: 0 us -> 158 us
  matrix products: 61.5 us -> 0 us
  waiting for transfers between devices: 231 us -> 184 us
  other arithmetic: 36.9 us -> 2.57 us
  local copies, waits for them, and re-layouts: 33.5 us -> 9.21 us
  starting transfers between devices: 12.1 us -> 5.67 us
    pallas_call x0 -> x3, Pallas kernels: none -> 158 us  [the longest x1 129 us: pack_pages(): pl.pallas_call(pack_kernel, out_shape=jax.ShapeDtypeStruct((count,) + pag...]
    psum x1 -> x0, waiting for transfers between devices: 101 us -> none  [body(): summed = lax.psum(partial_kv, 'tensor')]
    all_to_all x1, waiting for transfers between devices: 0.01 us -> 90.5 us  [body(): lax.all_to_all(outgoing, STORE, split_axis=0, concat_axis=0, tiled=True)]
    dot_general x7 -> x0, matrix products: 61.5 us -> none  [the longest x2 23.6 us: blend_attend(): jnp.einsum('hgqk,khd->qhgd', weights, key_value[:, :, 1], preferred_eleme...]
    all_gather x1, waiting for transfers between devices: 130 us -> 93.2 us  [gather_weight(): return lax.all_gather(weight_t, STORE, axis=0, tiled=True)]
    reduce_sum x4 -> x1, other arithmetic: 23.4 us -> 0.15 us  [body(): span_at = jnp.sum(at_rank * jnp.arange(spans)[None, None, :], axis=2)]
    gather x2 -> x0, local copies, waits for them, and re-layouts: 7.21 us -> none  [the longest x1 4.33 us: body(): outgoing = jnp.take(pages, source_slot.reshape(-1), axis=0)]
    while x6 -> x0, local copies, waits for them, and re-layouts: 7.08 us -> none
  transfers between devices with their start and end apart: 3 -> 3, of which waited for: 2 -> 2; matrix products, arithmetic and copies ran while one was open for 7% -> 1% of each run, Pallas kernels for 0% -> 35%
where the time goes in v1:
time: 378 us; the launch traced here: 374 us
  waiting for transfers between devices  184 us (49%)
  Pallas kernels  158 us (42%)
  between operations  14.2 us (4%)
  local copies, waits for them, and re-layouts  9.21 us (2%)
  starting transfers between devices  5.67 us (2%)
    pallas_call x1, Pallas kernels, pack_pages(): pl.pallas_call(pack_kernel, out_shape=jax.ShapeDtypeStruct((count,) + pag...  129 us
    all_gather x1, waiting for transfers between devices, gather_weight(): return lax.all_gather(weight_t, STORE, axis=0, tiled=True)  93.2 us
    all_to_all x1, waiting for transfers between devices, body(): lax.all_to_all(outgoing, STORE, split_axis=0, concat_axis=0, tiled=True)  90.5 us
    pallas_call x1, Pallas kernels, attend(): pl.pallas_call(functools.partial(attend_kernel, spans, per_span), out_sha...  20.6 us
    unnamed x18, local copies, waits for them, and re-layouts  8.23 us
    pallas_call x1, Pallas kernels, project(): pl.pallas_call(project_kernel, grid=(columns // block,), out_shape=jax.Sh...  8.13 us
  transfers between devices with their start and end apart: 3, of which 2 were waited for; matrix products, arithmetic and copies ran while one was open for 1% of the time, Pallas kernels for 35%

profile of v1, /device:TPU:1, one launch (start us, length us, event | category | flops | bytes accessed | tf_op | source)
XLA Modules:
  0.0 374.2 jit_solution(10568856825605203265)
XLA Ops:
  7.2 0.0 all-gather.2.cloned.1.call-start
  7.2 0.7 all-gather.2.cloned.1.call-update
  7.9 0.0 reduce-scatter.2.cloned.1.call-start
  7.9 0.8 copy.16
  8.7 0.8 copy.18
  9.5 93.2 %all-gather.2.cloned.1.call-done.weight_ref = bf16[2048,1536]{1,0:T(8,128)(2,1)} async-done(((bf16[64,1536]{1,0:T(8,128)(2,1)}), bf16[2048,1536]{1,0:T(8,128)(2,1)}) %all-gather.2.cloned.1.call-update) | async-done | bytes 6291472 | tf_op jit(solution)/shard_map/all_gather | solution.py:234
  102.7 0.0 copy-start.4
  102.7 2.8 copy-done.4
  105.5 0.0 copy-start.5
  105.5 1.9 copy-done.5
  107.4 8.1 %shard_map.104 = bf16[8,1024,256]{2,1,0:T(8,128)(2,1)S(1)} custom-call(bf16[1024,1536]{1,0:T(8,128)(2,1)S(1)} %copy-done.5, bf16[2048,1536]{1,0:T(8,128)(2,1)S(1)} %copy-done.4), custom_call_target="tpu_custom_call" | custom-call | flops 6442450944 | bytes 13631488 | tf_op jit(solution)/shard_map/pallas_call | solution.py:64
  115.5 0.0 copy-start
  115.5 2.0 copy-done
  117.5 0.0 reduce-scatter.2.cloned.1.call-update
  117.5 0.1 select_reduce_fusion.1
  117.7 0.1 reduce_min.14
  117.8 0.1 reduce_max.14
  117.9 0.1 reduce_min.18
  118.0 0.1 reduce_max.18
  118.1 0.1 copy.19
  118.2 0.1 reshape.75
  118.3 0.5 and_select_fusion.slot_ref
  118.8 129.4 %shard_map.105 = bf16[64,128,256]{2,1,0:T(8,128)(2,1)} custom-call(s32[64]{0:T(128)} %and_select_fusion.slot_ref, bf16[32,128,256]{2,1,0:T(8,128)(2,1)} %pages_ref.1), custom_call_target="tpu_custom_call" | custom-call | bytes 8388608 | tf_op jit(solution)/shard_map/pallas_call | solution.py:40
  248.3 0.0 copy-start.2
  248.3 0.0 copy-start.3
  248.3 0.0 copy-start.7
  248.3 0.0 copy-start.6
  248.3 5.6 %all-to-all-start = ((bf16[32,2,128,256]{3,2,1,0:T(8,128)(2,1)}), bf16[32,2,128,256]{3,2,1,0:T(8,128)(2,1)}, u32[]{:S(2)}, u32[]{:S(2)}) async-start(bf16[32,2,128,256]{3,2,1,0:T(8,128)(2,1)} %bitcast.12), calls=%async_computation.1 | async-start | bytes 8388608 | tf_op jit(solution)/shard_map/all_to_all | solution.py:255
  253.9 0.1 reshape.72
  254.0 0.0 copy-done.2
  254.0 0.1 broadcast_in_dim.38
  254.0 0.0 copy-done.3
  254.1 0.1 iota_compare_fusion
  254.1 0.1 lt.50
  254.2 0.2 fusion.1
  254.4 0.1 reshape.78
  254.5 0.1 mul.46
  254.6 0.0 copy-done.7
  254.6 0.2 select_reduce_fusion.2
  254.8 0.0 reduce-scatter.2.cloned.1.call-done
  254.8 1.2 bitcast_select_fusion.new_ref
  256.0 0.0 copy-start.1
  256.1 90.5 %all-to-all-done = bf16[32,2,128,256]{3,2,1,0:T(8,128)(2,1)} async-done(((bf16[32,2,128,256]{3,2,1,0:T(8,128)(2,1)}), bf16[32,2,128,256]{3,2,1,0:T(8,128)(2,1)}, u32[]{:S(2)}, u32[]{:S(2)}) %all-to-all-start) | async-done | bytes 4194336 | tf_op jit(solution)/shard_map/all_to_all | solution.py:255
  346.5 0.2 broadcast_in_dim.39.pos_lane_ref
  346.7 0.0 copy-done.6
  346.7 20.6 %shard_map.106 = bf16[1024,768]{1,0:T(8,128)(2,1)} custom-call(s32[2,16]{1,0:T(2,128)S(1)} %get-tuple-element.5.page_ref, s32[2,16]{1,0:T(2,128)S(1)} %get-tuple-element.4.span_ref, s32[2,16]{1,0:T(2,128)S(1)} %copy-done.3, bf16[1024,768]{1,0:T(8,128)(2,1)S(1)} %copy-done.6, bf16[1024,256]{1,0:T(8,128)(2,1)S(1)} %bitcast_select_fusion.new_ref, ...), custom_call_target="tpu_custom_call" | custom-call | flops 4831838208 | bytes 7340032 | tf_op jit(solution)/shard_map/pallas_call | solution.py:211
  367.3 0.0 copy-done.1
  (6 shorter events, 0.1 us)
Async XLA Ops:
  7.2 95.5 %all-gather.2.cloned.1.call-start = ((), (), s32[]{:S(2)}) async-start(), calls=%async_computation.2 | async-start | bytes 6488064 | tf_op jit(solution)/shard_map/all_gather | solution.py:234
  7.9 246.9 %reduce-scatter.2.cloned.1.call-start = ((), (), s32[]{:S(2)}) async-start(), calls=%async_computation.3 | async-start | bytes 4718592 | tf_op jit(solution)/shard_map/reduce_scatter | solution.py:260
  102.7 2.8 copy-start.4
  105.5 1.9 copy-start.5
  115.5 2.0 copy-start
  248.3 5.7 %copy-start.2 = (s32[2,16,32]{2,1,0:T(8,128)S(1)}, s32[2,16,32]{2,1,0:T(8,128)}, u32[]{:S(2)}) copy-start(s32[2,16,32]{2,1,0:T(8,128)} %param.16) | copy-start | bytes 12292
  248.3 5.8 %copy-start.3 = (s32[2,16]{1,0:T(2,128)S(1)}, s32[2,16]{1,0:T(2,128)}, u32[]{:S(2)}) copy-start(s32[2,16]{1,0:T(2,128)} %count_ref.1) | copy-start | bytes 388
  248.3 6.3 %copy-start.7 = (s32[2,16]{1,0:T(2,128)S(1)}, s32[2,16]{1,0:T(2,128)}, u32[]{:S(2)}) copy-start(s32[2,16]{1,0:T(2,128)} %param.15) | copy-start | bytes 388
  248.3 98.4 %copy-start.6 = (bf16[1024,768]{1,0:T(8,128)(2,1)S(1)}, bf16[1024,768]{1,0:T(8,128)(2,1)}, u32[]{:S(2)}) copy-start(bf16[1024,768]{1,0:T(8,128)(2,1)} %q_ref.1) | copy-start | bytes 4718596
  248.3 98.2 %all-to-all-start = ((bf16[32,2,128,256]{3,2,1,0:T(8,128)(2,1)}), bf16[32,2,128,256]{3,2,1,0:T(8,128)(2,1)}, u32[]{:S(2)}, u32[]{:S(2)}) async-start(bf16[32,2,128,256]{3,2,1,0:T(8,128)(2,1)} %bitcast.12), calls=%async_computation.1 | async-start | bytes 8388608 | tf_op jit(solution)/shard_map/all_to_all | solution.py:255
  256.0 111.3 %copy-start.1 = (bf16[1024,256]{1,0:T(8,128)(2,1)}, bf16[1024,256]{1,0:T(8,128)(2,1)S(1)}, u32[]{:S(2)}) copy-start(bf16[1024,256]{1,0:T(8,128)(2,1)S(1)} %bitcast_select_fusion.new_ref) | copy-start | bytes 1572868
Sparse Core Ops, SparseCore 0:
  10.6 92.0 all-gather.1
  117.6 34.9 reduce-scatter.1

commit v2 on v1

--- a/solution.py
+++ b/solution.py
@@ -44,39 +44,64 @@
             pl.BlockSpec(memory_space=pltpu.SMEM),
             pl.BlockSpec(memory_space=pl.ANY),
         ],
-        out_specs=pl.BlockSpec(memory_space=pl.ANY),
+        out_specs=pl.BlockSpec(memory_space=pltpu.VMEM),
         scratch_shapes=[pltpu.SemaphoreType.DMA((count,))],
-        cost_estimate=pl.CostEstimate(
-            flops=0, bytes_accessed=4 * count * pages.shape[1] * pages.shape[2], transcendentals=0
-        ),
+        cost_estimate=pl.CostEstimate(flops=0, bytes_accessed=1024, transcendentals=0),
     )(source_slot, pages)
 
 
-def project_kernel(hidden_ref, weight_ref, out_ref):
-    out_ref[0] = lax.dot_general(
-        hidden_ref[...], weight_ref[...], (((1,), (1,)), ((), ())), preferred_element_type=F32
-    ).astype(out_ref.dtype)
-
-
-def project(hidden, weight_t, block):
-    rows, width = hidden.shape
-    columns = weight_t.shape[0]
+def project_kernel(slot_ref, own_ref, other_ref, *rest):
+    weights = rest[:4]
+    outs = rest[4:8]
+    held, sems = rest[8:]
+    halves, slices, columns, width = weights[0].shape
+    block = halves * columns
+    copies = []
+    for i in range(4):
+        for j in range(halves):
+            for s in range(slices):
+                at = pl.multiple_of(slot_ref[i] * block + j * columns, columns)
+                copies.append(
+                    pltpu.make_async_copy(
+                        weights[i].at[j, s], held.at[s, pl.ds(at, columns)], sems.at[i, j, s]
+                    )
+                )
+    for copy in copies:
+        copy.start()
+    for copy in copies:
+        copy.wait()
+    step = 256
+    for row in range(0, own_ref.shape[0], step):
+        rows = slice(row, row + step)
+        product = sum(
+            lax.dot_general(
+                ref[rows, :], held[s], (((1,), (1,)), ((), ())), preferred_element_type=F32
+            )
+            for s, ref in enumerate((own_ref, other_ref))
+        )
+        for i in range(4):
+            outs[i][rows, :] = product[:, i * block : (i + 1) * block].astype(BF16)
+
+
+def project(slots, own, other, weights):
+    rows, width = own.shape
+    halves, slices, columns, _ = weights[0].shape
+    block = halves * columns
+    vmem = pl.BlockSpec(memory_space=pltpu.VMEM)
+    in_specs = [pl.BlockSpec(memory_space=pltpu.SMEM), vmem, vmem]
+    in_specs += [pl.BlockSpec(memory_space=pl.ANY)] * 4
     return pl.pallas_call(
         project_kernel,
-        grid=(columns // block,),
-        out_shape=jax.ShapeDtypeStruct((columns // block, rows, block), BF16),
-        in_specs=[
-            pl.BlockSpec((rows, width), lambda i: (0, 0)),
-            pl.BlockSpec((block, width), lambda i: (i, 0)),
+        out_shape=[jax.ShapeDtypeStruct((rows, block), BF16)] * 4,
+        in_specs=in_specs,
+        out_specs=[vmem] * 4,
+        scratch_shapes=[
+            pltpu.VMEM((slices, 4 * block, width), BF16),
+            pltpu.SemaphoreType.DMA((4, halves, slices)),
         ],
-        out_specs=pl.BlockSpec((1, rows, block), lambda i: (i, 0, 0)),
         compiler_params=pltpu.CompilerParams(vmem_limit_bytes=40 << 20),
-        cost_estimate=pl.CostEstimate(
-            flops=2 * rows * width * columns,
-            bytes_accessed=2 * (rows * width + columns * width + rows * columns),
-            transcendentals=0,
-        ),
-    )(hidden, weight_t)
+        cost_estimate=pl.CostEstimate(flops=0, bytes_accessed=1024, transcendentals=0),
+    )(slots, own, other, *weights)
 
 
 def attend_kernel(
@@ -222,16 +247,50 @@
             pltpu.SemaphoreType.DMA((requests, spans)),
         ],
         compiler_params=pltpu.CompilerParams(vmem_limit_bytes=48 << 20),
-        cost_estimate=pl.CostEstimate(
-            flops=2 * requests * pair * length * HEAD * 3 * spans // 4,
-            bytes_accessed=4 * queries.size + 2 * arrived.size,
-            transcendentals=requests * pair * length * spans // 4,
-        ),
+        cost_estimate=pl.CostEstimate(flops=0, bytes_accessed=1024, transcendentals=0),
     )(page_at, span_at, counts, queries, new_kv, pos_row, pos_lane, arrived)
 
 
-def gather_weight(weight_t):
-    return lax.all_gather(weight_t, STORE, axis=0, tiled=True)
+def shift(x, axis, by):
+    size = lax.axis_size(axis)
+    return lax.ppermute(x, axis, [(i, (i + by) % size) for i in range(size)])
+
+
+def gather_over_z(pair):
+    z = lax.axis_index("z")
+    core = lax.axis_index("core")
+    gathered = jnp.zeros((4,) + pair.shape, BF16)
+    for by in range(4):
+        near = []
+        for hop in (by, by + 4):
+            moves = [(s * 2 + s // 4, (s + hop) % 8 * 2 + s // 4) for s in range(8)]
+            near.append(lax.ppermute(pair, ("z", "core"), moves) if hop else pair)
+        first = (z - by) % 8 // 4 == core
+        piece = jnp.where(first, near[0], near[1])
+        gathered = lax.dynamic_update_slice(gathered, piece[None], ((z - by) % 4, 0, 0, 0))
+    return gathered
+
+
+def new_rows(hidden, gathered):
+    ahead = (lax.axis_index("x") - lax.axis_index("y") - jnp.arange(4)) % 4
+    other = shift(hidden, "core", 1)
+    parts = []
+    for part in range(2):
+        piece = gathered[2 * part : 2 * part + 2]
+        parts.append([piece] + [shift(piece, "x", by) for by in (1, 2, 3)])
+    totals = []
+    for weights in parts:
+        if totals:
+            weights[0], products = lax.optimization_barrier((weights[0], products))
+            received = [shift(products[by], "y", by) for by in (1, 3, 2)]
+            totals[0] = sum((p.astype(F32) for p in received), products[0].astype(F32))
+        products = project(ahead, hidden, other, weights)
+        if not totals:
+            totals.append(None)
+        else:
+            received = [shift(products[by], "y", by) for by in (1, 3, 2)]
+            totals.append(sum((p.astype(F32) for p in received), products[0].astype(F32)))
+    return jnp.concatenate(totals, axis=1)
 
 
 def body(hidden, kv_weight, pages, queries, page_owner, page_slot, span_order, positions, counts):
@@ -251,21 +310,25 @@
     first = jnp.min(jnp.where(mine, code, entries * pages.shape[0]), axis=1)
     last = jnp.max(jnp.where(mine, code, 0), axis=1)
     source_slot = jnp.stack([first, last], axis=1).reshape(-1) % pages.shape[0]
-    outgoing = pack_pages(source_slot, pages).reshape(stores, 2, span_len, kv_width)
-    arrived = lax.all_to_all(outgoing, STORE, split_axis=0, concat_axis=0, tiled=True)
+    outgoing = pack_pages(source_slot, pages)
+    shard, outgoing = lax.optimization_barrier((kv_weight.T, outgoing))
+    pair = jnp.stack([shard, shift(shard, "core", 1)])
+    gathered = gather_over_z(pair)
+    outgoing = outgoing.reshape(4, 8, 2, span_len, kv_width)
+    halfway = lax.all_to_all(outgoing, "x", split_axis=0, concat_axis=0, tiled=True)
+    halfway = halfway.transpose(1, 0, 2, 3, 4)
+    halfway, gathered = lax.optimization_barrier((halfway, gathered))
+    arrived = lax.all_to_all(halfway, "z", split_axis=0, concat_axis=0, tiled=True)
     arrived = arrived.reshape(stores * 2, span_len, kv_width)
 
-    weight_t = gather_weight(kv_weight.T)
-    partial_kv = project(hidden, weight_t, kv_width)
-    own_kv = lax.psum_scatter(partial_kv, TENSOR, scatter_dimension=0, tiled=True)
-    own_kv = own_kv.reshape(entries * per_span, kv_width)
+    own_kv = new_rows(hidden, gathered)
     row_used = jnp.arange(per_span)[None, None, :] < counts[:, :, None]
-    new_kv = jnp.where(row_used.reshape(-1, 1), own_kv, jnp.zeros((), BF16))
+    new_kv = jnp.where(row_used.reshape(-1, 1), own_kv, 0.0).astype(BF16)
 
     my_owner = lax.dynamic_index_in_dim(owners, store_index, 0, keepdims=False)
     earlier = jnp.arange(entries)[None, :] < jnp.arange(entries)[:, None]
     second = jnp.any((my_owner[:, None] == my_owner[None, :]) & earlier, axis=1)
-    page_of = (my_owner * 2 + second.astype(jnp.int32)).reshape(requests, spans)
+    page_of = ((my_owner % 8 * 4 + my_owner // 8) * 2 + second.astype(jnp.int32)).reshape(requests, spans)
     at_rank = span_order[:, None, :] == jnp.arange(spans)[None, :, None]
     span_at = jnp.sum(at_rank * jnp.arange(spans)[None, None, :], axis=2)
     page_at = jnp.sum(at_rank * page_of[:, None, :], axis=2)

time: 378 us -> 201 us (0.53)
  Pallas kernels: 158 us -> 41 us
  waiting for transfers between devices: 184 us -> 83.4 us
  starting transfers between devices: 5.67 us -> 46.3 us
  between operations: 14.2 us -> 1.33 us
  local copies, waits for them, and re-layouts: 9.21 us -> 20.7 us
  other arithmetic: 2.57 us -> 7.26 us
    pallas_call x1, Pallas kernels: 129 us -> 6.26 us  [pack_pages(): pl.pallas_call(pack_kernel, out_shape=jax.ShapeDtypeStruct((count,) + pag...]
    all_gather x1 -> x0, waiting for transfers between devices: 93.2 us -> none  [gather_weight(): return lax.all_gather(weight_t, STORE, axis=0, tiled=True)]
    all_to_all x1 -> x2, waiting for transfers between devices: 90.5 us -> 3.38 us  [the longest x1 3.38 us: body(): lax.all_to_all(outgoing, 'x', split_axis=0, concat_axis=0, tiled=True)]
    ppermute x0 -> x21, waiting for transfers between devices: none -> 80 us  [the longest x14 53.4 us: shift(): return lax.ppermute(x, axis, [(i, (i + by) % size) for i in range(size)])]
    ppermute x0 -> x21, starting transfers between devices: none -> 30.8 us  [the longest x14 23.6 us: shift(): return lax.ppermute(x, axis, [(i, (i + by) % size) for i in range(size)])]
    all_to_all x1 -> x2, starting transfers between devices: 5.59 us -> 15.5 us  [the longest x1 10.5 us: body(): lax.all_to_all(halfway, 'z', split_axis=0, concat_axis=0, tiled=True)]
    pallas_call x1 -> x2, Pallas kernels: 8.13 us -> 14 us  [project(): pl.pallas_call(project_kernel, out_shape=[jax.ShapeDtypeStruct((rows, blo...]
    optimization_barrier x0 -> x1, local copies, waits for them, and re-layouts: none -> 4.62 us  [body(): halfway, gathered = lax.optimization_barrier((halfway, gathered))]
  transfers between devices with their start and end apart: 3 -> 23, of which waited for: 2 -> 13; matrix products, arithmetic and copies ran while one was open for 1% -> 5% of each run, Pallas kernels for 35% -> 7%
where the time goes in v2:
time: 201 us; the launch traced here: 200 us
  waiting for transfers between devices  83.4 us (41%)
  starting transfers between devices  46.3 us (23%)
  Pallas kernels  41 us (20%)
  local copies, waits for them, and re-layouts  20.7 us (10%)
  other arithmetic  7.26 us (4%)
    ppermute x14, waiting for transfers between devices, shift(): return lax.ppermute(x, axis, [(i, (i + by) % size) for i in range(size)])  53.4 us
    ppermute x7, waiting for transfers between devices, gather_over_z(): near.append(lax.ppermute(pair, ('z', 'core'), moves) if hop else pair)  26.7 us
    ppermute x14, starting transfers between devices, shift(): return lax.ppermute(x, axis, [(i, (i + by) % size) for i in range(size)])  23.6 us
    pallas_call x1, Pallas kernels, attend(): pl.pallas_call(functools.partial(attend_kernel, spans, per_span), out_sha...  20.8 us
    pallas_call x2, Pallas kernels, project(): pl.pallas_call(project_kernel, out_shape=[jax.ShapeDtypeStruct((rows, blo...  14 us
    unnamed x32, local copies, waits for them, and re-layouts  11.2 us
    all_to_all x1, starting transfers between devices, body(): lax.all_to_all(halfway, 'z', split_axis=0, concat_axis=0, tiled=True)  10.5 us
    ppermute x7, starting transfers between devices, gather_over_z(): near.append(lax.ppermute(pair, ('z', 'core'), moves) if hop else pair)  7.2 us
  transfers between devices with their start and end apart: 23, of which 13 were waited for; matrix products, arithmetic and copies ran while one was open for 5% of the time, Pallas kernels for 7%

profile of v2, /device:TPU:1, one launch (start us, length us, event | category | flops | bytes accessed | tf_op | source)
XLA Modules:
  0.0 200.1 jit_solution(1374070044222768458)
XLA Ops:
  3.5 6.3 %shard_map.104 = bf16[64,128,256]{2,1,0:T(8,128)(2,1)} custom-call(s32[64]{0:T(128)} %and_select_fusion.1.slot_ref, bf16[32,128,256]{2,1,0:T(8,128)(2,1)} %pages_ref.1), custom_call_target="tpu_custom_call" | custom-call | bytes 1024 | tf_op jit(solution)/shard_map/pallas_call | solution.py:40
  9.8 5.0 %all-to-all-start = ((bf16[4,8,2,128,256]{4,3,2,1,0:T(8,128)(2,1)}), bf16[4,8,2,128,256]{4,3,2,1,0:T(8,128)(2,1)}, u32[]{:S(2)}, u32[]{:S(2)}) async-start(bf16[4,8,2,128,256]{4,3,2,1,0:T(8,128)(2,1)} %bitcast.21), calls=%async_computation | async-start | bytes 8388608 | tf_op jit(solution)/shard_map/all_to_all | solution.py:318
  14.8 3.3 %collective-permute-start = (bf16[64,1536]{1,0:T(8,128)(2,1)S(1)}, bf16[64,1536]{1,0:T(8,128)(2,1)S(1)}, u32[]{:S(2)}, u32[]{:S(2)}) collective-permute-start(bf16[64,1536]{1,0:T(8,128)(2,1)S(1)} %bitcast.22), channel_id=1, source_target_pairs={{0,1},{1,0},{2,3},{3,2},{4,5},{5,4},{6,7},{7,6},{8,9},{9,8},{10,11... | collective-permute-start | bytes 589832 | tf_op jit(solution)/shard_map/ppermute | solution.py:256
  18.2 1.1 collective-permute-done
  19.3 1.3 collective-permute-start.1
  20.8 1.3 collective-permute-start.2
  22.8 1.3 collective-permute-start.4
  24.8 7.2 %collective-permute-done.1 = bf16[2,64,1536]{2,1,0:T(8,128)(2,1)S(1)} collective-permute-done((bf16[2,64,1536]{2,1,0:T(8,128)(2,1)S(1)}, bf16[2,64,1536]{2,1,0:T(8,128)(2,1)S(1)}, u32[]{:S(2)}, u32[]{:S(2)}) %collective-permute-start.1) | collective-permute-done | bytes 393248 | tf_op jit(solution)/shard_map/ppermute | solution.py:267
  31.9 1.3 collective-permute-start.6
  33.2 1.3 broadcast_in_dim.54
  35.3 4.2 %collective-permute-done.2 = bf16[2,64,1536]{2,1,0:T(8,128)(2,1)S(1)} collective-permute-done((bf16[2,64,1536]{2,1,0:T(8,128)(2,1)S(1)}, bf16[2,64,1536]{2,1,0:T(8,128)(2,1)S(1)}, u32[]{:S(2)}, u32[]{:S(2)}) %collective-permute-start.2) | collective-permute-done | bytes 393248 | tf_op jit(solution)/shard_map/ppermute | solution.py:267
  40.2 0.8 bitcast_dynamic-update-slice_fusion.2
  41.0 2.6 %collective-permute-done.4 = bf16[2,64,1536]{2,1,0:T(8,128)(2,1)S(1)} collective-permute-done((bf16[2,64,1536]{2,1,0:T(8,128)(2,1)S(1)}, bf16[2,64,1536]{2,1,0:T(8,128)(2,1)S(1)}, u32[]{:S(2)}, u32[]{:S(2)}) %collective-permute-start.4) | collective-permute-done | bytes 393248 | tf_op jit(solution)/shard_map/ppermute | solution.py:267
  43.7 0.8 bitcast_dynamic-update-slice_fusion.1
  44.5 12.7 %collective-permute-done.6 = bf16[2,64,1536]{2,1,0:T(8,128)(2,1)S(1)} collective-permute-done((bf16[2,64,1536]{2,1,0:T(8,128)(2,1)S(1)}, bf16[2,64,1536]{2,1,0:T(8,128)(2,1)S(1)}, u32[]{:S(2)}, u32[]{:S(2)}) %collective-permute-start.6) | collective-permute-done | bytes 393248 | tf_op jit(solution)/shard_map/ppermute | solution.py:267
  57.2 0.8 bitcast_dynamic-update-slice_fusion
  58.1 3.4 %all-to-all-done = bf16[4,8,2,128,256]{4,3,2,1,0:T(8,128)(2,1)} async-done(((bf16[4,8,2,128,256]{4,3,2,1,0:T(8,128)(2,1)}), bf16[4,8,2,128,256]{4,3,2,1,0:T(8,128)(2,1)}, u32[]{:S(2)}, u32[]{:S(2)}) %all-to-all-start) | async-done | bytes 4194336 | tf_op jit(solution)/shard_map/all_to_all | solution.py:318
  61.4 4.6 %copy.32 = bf16[8,4,2,128,256]{4,3,2,1,0:T(8,128)(2,1)} copy(bf16[8,4,2,128,256]{4,3,2,0,1:T(8,128)(2,1)} %bitcast.6) | data formatting | bytes 8388608 | tf_op jit(solution)/shard_map/optimization_barrier | solution.py:320
  66.1 10.5 %all-to-all-start.1 = ((bf16[8,4,2,128,256]{4,3,2,1,0:T(8,128)(2,1)}), bf16[8,4,2,128,256]{4,3,2,1,0:T(8,128)(2,1)}, u32[]{:S(2)}, u32[]{:S(2)}) async-start(bf16[8,4,2,128,256]{4,3,2,1,0:T(8,128)(2,1)} %copy.32), calls=%async_computation.1 | async-start | bytes 8388608 | tf_op jit(solution)/shard_map/all_to_all | solution.py:321
  76.6 1.9 collective-permute-start.8
  78.5 2.6 %fusion.9 = (bf16[2,2,64,1536]{3,2,1,0:T(8,128)(2,1)}, bf16[2,2,64,1536]{3,2,1,0:T(8,128)(2,1)}) fusion(bf16[4,2,64,1536]{3,2,1,0:T(8,128)(2,1)} %bitcast_dynamic-update-slice_fusion), kind=kLoop, calls=%fused_computation.40 | loop fusion | bytes 3145728 | tf_op jit(solution)/shard_map/slice | solution.py:279
  81.1 0.9 collective-permute-start.10
  82.0 2.0 collective-permute-start.11
  84.7 1.7 copy-done.1
  86.4 3.2 %collective-permute-start.16 = (bf16[2,2,64,1536]{3,2,1,0:T(8,128)(2,1)}, bf16[2,2,64,1536]{3,2,1,0:T(8,128)(2,1)}, u32[]{:S(2)}, u32[]{:S(2)}) collective-permute-start(bf16[2,2,64,1536]{3,2,1,0:T(8,128)(2,1)} %get-tuple-element.30.rest_0_), channel_id=1, source_target_pairs={{0,128},{64,192},{128,0},{192,64},{1,129},{65,193},{129,1},{193,65... | collective-permute-start | bytes 2359304 | tf_op jit(solution)/shard_map/ppermute | solution.py:256
  89.5 12.6 %collective-permute-done.10.rest_2_ = bf16[2,2,64,1536]{3,2,1,0:T(8,128)(2,1)S(1)} collective-permute-done((bf16[2,2,64,1536]{3,2,1,0:T(8,128)(2,1)}, bf16[2,2,64,1536]{3,2,1,0:T(8,128)(2,1)S(1)}, u32[]{:S(2)}, u32[]{:S(2)}) %collective-permute-start.10) | collective-permute-done | bytes 786464 | tf_op jit(solution)/shard_map/ppermute | solution.py:256
  102.1 0.9 copy-done.6
  103.0 1.5 collective-permute-start.17
  104.7 13.4 %collective-permute-done.11.rest_3_ = bf16[2,2,64,1536]{3,2,1,0:T(8,128)(2,1)} collective-permute-done((bf16[2,2,64,1536]{3,2,1,0:T(8,128)(2,1)}, bf16[2,2,64,1536]{3,2,1,0:T(8,128)(2,1)}, u32[]{:S(2)}, u32[]{:S(2)}) %collective-permute-start.11) | collective-permute-done | bytes 786464 | tf_op jit(solution)/shard_map/ppermute | solution.py:256
  118.1 1.1 collective-permute-done.9.rest_1_
  119.2 1.9 copy-done.2
  121.1 1.1 copy-done.7
  122.2 7.0 %shard_map.105 = (bf16[1024,128]{1,0:T(8,128)(2,1)S(1)}, bf16[1024,128]{1,0:T(8,128)(2,1)}, bf16[1024,128]{1,0:T(8,128)(2,1)S(1)}, bf16[1024,128]{1,0:T(8,128)(2,1)S(1)}) custom-call(s32[4]{0:T(128)S(1)} %and_select_fusion.slot_ref, bf16[1024,1536]{1,0:T(8,128)(2,1)S(1)} %copy-done, bf16[1024,1536]{1,0:T(8,128)(2,1)S(1)} %copy-done.2, ...), custom_call_target="tpu_custom_call" | custom-call | bytes 1024 | tf_op jit(solution)/shard_map/pallas_call | solution.py:93
  130.7 1.3 collective-permute-start.12
  132.3 1.6 collective-permute-start.13
  133.9 2.4 %collective-permute-done.15.rest_1_ = bf16[2,2,64,1536]{3,2,1,0:T(8,128)(2,1)} collective-permute-done((bf16[2,2,64,1536]{3,2,1,0:T(8,128)(2,1)}, bf16[2,2,64,1536]{3,2,1,0:T(8,128)(2,1)}, u32[]{:S(2)}, u32[]{:S(2)}) %collective-permute-start.15) | collective-permute-done | bytes 786464 | tf_op jit(solution)/shard_map/ppermute | solution.py:256
  136.3 2.9 %collective-permute-start.14 = (bf16[1024,128]{1,0:T(8,128)(2,1)}, bf16[1024,128]{1,0:T(8,128)(2,1)}, u32[]{:S(2)}, u32[]{:S(2)}) collective-permute-start(bf16[1024,128]{1,0:T(8,128)(2,1)} %copy-done.11), channel_id=1, source_target_pairs={{0,4},{2,6},{4,0},{6,2},{1,5},{3,7},{5,1},{7,3},{8,12},{10,14},{12... | collective-permute-start | bytes 786440 | tf_op jit(solution)/shard_map/ppermute | solution.py:256
  139.3 13.4 %collective-permute-done.16.rest_2_ = bf16[2,2,64,1536]{3,2,1,0:T(8,128)(2,1)} collective-permute-done((bf16[2,2,64,1536]{3,2,1,0:T(8,128)(2,1)}, bf16[2,2,64,1536]{3,2,1,0:T(8,128)(2,1)}, u32[]{:S(2)}, u32[]{:S(2)}) %collective-permute-start.16) | collective-permute-done | bytes 786464 | tf_op jit(solution)/shard_map/ppermute | solution.py:256
  152.7 1.9 copy-done.3
  154.6 6.9 %shard_map.106 = (bf16[1024,128]{1,0:T(8,128)(2,1)S(1)}, bf16[1024,128]{1,0:T(8,128)(2,1)}, bf16[1024,128]{1,0:T(8,128)(2,1)}, bf16[1024,128]{1,0:T(8,128)(2,1)}) custom-call(s32[4]{0:T(128)S(1)} %and_select_fusion.slot_ref, bf16[1024,1536]{1,0:T(8,128)(2,1)S(1)} %copy-done, bf16[1024,1536]{1,0:T(8,128)(2,1)S(1)} %copy-done.3, ...), custom_call_target="tpu_custom_call" | custom-call | bytes 1024 | tf_op jit(solution)/shard_map/pallas_call | solution.py:93
  162.2 1.3 collective-permute-start.18
  163.5 1.4 collective-permute-start.19
  165.0 1.6 collective-permute-start.20
  166.9 1.3 convert_add_fusion.1
  168.2 2.7 %collective-permute-done.18 = bf16[1024,128]{1,0:T(8,128)(2,1)S(1)} collective-permute-done((bf16[1024,128]{1,0:T(8,128)(2,1)}, bf16[1024,128]{1,0:T(8,128)(2,1)S(1)}, u32[]{:S(2)}, u32[]{:S(2)}) %collective-permute-start.18) | collective-permute-done | bytes 262176 | tf_op jit(solution)/shard_map/ppermute | solution.py:256
  170.9 6.6 %collective-permute-done.20 = bf16[1024,128]{1,0:T(8,128)(2,1)S(1)} collective-permute-done((bf16[1024,128]{1,0:T(8,128)(2,1)}, bf16[1024,128]{1,0:T(8,128)(2,1)S(1)}, u32[]{:S(2)}, u32[]{:S(2)}) %collective-permute-start.20) | collective-permute-done | bytes 262176 | tf_op jit(solution)/shard_map/ppermute | solution.py:256
  177.6 1.1 convert_add_fusion
  179.1 20.8 %shard_map.107 = bf16[1024,768]{1,0:T(8,128)(2,1)} custom-call(s32[2,16]{1,0:T(2,128)S(1)} %get-tuple-element.39.page_ref, s32[2,16]{1,0:T(2,128)S(1)} %get-tuple-element.38.span_ref, s32[2,16]{1,0:T(2,128)S(1)} %copy-done.10, bf16[1024,768]{1,0:T(8,128)(2,1)S(1)} %copy-done.5, bf16[1024,256]{1,0:T(8,128)(2,1)S(1)} %fusion.new_ref, s32[32,32]{1,0:T(8,128)S(1)} %bitcast.20, ...), custom_call_target="tpu_custom_call" | custom-call | bytes 1024 | tf_op jit(solution)/shard_map/pallas_call | solution.py:236
  (69 shorter events, 9.9 us)
Async XLA Ops:
  9.8 5.0 %copy-start.13 = (bf16[1536,64]{0,1:T(8,128)(2,1)S(1)}, bf16[1536,64]{0,1:T(8,128)(2,1)}, u32[]{:S(2)}) copy-start(bf16[1536,64]{0,1:T(8,128)(2,1)} %param.10) | copy-start | bytes 589828
  9.8 51.6 %all-to-all-start = ((bf16[4,8,2,128,256]{4,3,2,1,0:T(8,128)(2,1)}), bf16[4,8,2,128,256]{4,3,2,1,0:T(8,128)(2,1)}, u32[]{:S(2)}, u32[]{:S(2)}) async-start(bf16[4,8,2,128,256]{4,3,2,1,0:T(8,128)(2,1)} %bitcast.21), calls=%async_computation | async-start | bytes 8388608 | tf_op jit(solution)/shard_map/all_to_all | solution.py:318
  14.8 4.4 %collective-permute-start = (bf16[64,1536]{1,0:T(8,128)(2,1)S(1)}, bf16[64,1536]{1,0:T(8,128)(2,1)S(1)}, u32[]{:S(2)}, u32[]{:S(2)}) collective-permute-start(bf16[64,1536]{1,0:T(8,128)(2,1)S(1)} %bitcast.22), channel_id=1, source_target_pairs={{0,1},{1,0},{2,3},{3,2},{4,5},{5,4},{6,7},{7,6},{8,9},{9,8},{10,11... | collective-permute-start | bytes 589832 | tf_op jit(solution)/shard_map/ppermute | solution.py:256
  19.3 12.7 %collective-permute-start.1 = (bf16[2,64,1536]{2,1,0:T(8,128)(2,1)S(1)}, bf16[2,64,1536]{2,1,0:T(8,128)(2,1)S(1)}, u32[]{:S(2)}, u32[]{:S(2)}) collective-permute-start(bf16[2,64,1536]{2,1,0:T(8,128)(2,1)S(1)} %pad_maximum_fusion), channel_id=1, source_target_pairs={{0,32},{8,40},{16,48},{24,56},{33,1},{41,9},{49,17},{57,25},{2,34}... | collective-permute-start | bytes 1179656 | tf_op jit(solution)/shard_map/ppermute | solution.py:267
  20.8 18.7 %collective-permute-start.2 = (bf16[2,64,1536]{2,1,0:T(8,128)(2,1)S(1)}, bf16[2,64,1536]{2,1,0:T(8,128)(2,1)S(1)}, u32[]{:S(2)}, u32[]{:S(2)}) collective-permute-start(bf16[2,64,1536]{2,1,0:T(8,128)(2,1)S(1)} %pad_maximum_fusion), channel_id=1, source_target_pairs={{0,8},{8,16},{16,24},{24,32},{33,41},{41,49},{49,57},{57,1},{2,10}... | collective-permute-start | bytes 1179656 | tf_op jit(solution)/shard_map/ppermute | solution.py:267
  22.1 18.1 %collective-permute-start.3 = (bf16[2,64,1536]{2,1,0:T(8,128)(2,1)S(1)}, bf16[2,64,1536]{2,1,0:T(8,128)(2,1)S(1)}, u32[]{:S(2)}, u32[]{:S(2)}) collective-permute-start(bf16[2,64,1536]{2,1,0:T(8,128)(2,1)S(1)} %pad_maximum_fusion), channel_id=1, source_target_pairs={{0,40},{8,48},{16,56},{24,0},{33,9},{41,17},{49,25},{57,33},{2,42}... | collective-permute-start | bytes 1179656 | tf_op jit(solution)/shard_map/ppermute | solution.py:267
  22.8 20.9 %collective-permute-start.4 = (bf16[2,64,1536]{2,1,0:T(8,128)(2,1)S(1)}, bf16[2,64,1536]{2,1,0:T(8,128)(2,1)S(1)}, u32[]{:S(2)}, u32[]{:S(2)}) collective-permute-start(bf16[2,64,1536]{2,1,0:T(8,128)(2,1)S(1)} %pad_maximum_fusion), channel_id=1, source_target_pairs={{0,16},{8,24},{16,32},{24,40},{33,49},{41,57},{49,1},{57,9},{2,18}... | collective-permute-start | bytes 1179656 | tf_op jit(solution)/shard_map/ppermute | solution.py:267
  24.1 19.6 %collective-permute-start.5 = (bf16[2,64,1536]{2,1,0:T(8,128)(2,1)S(1)}, bf16[2,64,1536]{2,1,0:T(8,128)(2,1)S(1)}, u32[]{:S(2)}, u32[]{:S(2)}) collective-permute-start(bf16[2,64,1536]{2,1,0:T(8,128)(2,1)S(1)} %pad_maximum_fusion), channel_id=1, source_target_pairs={{0,48},{8,56},{16,0},{24,8},{33,17},{41,25},{49,33},{57,41},{2,50}... | collective-permute-start | bytes 1179656 | tf_op jit(solution)/shard_map/ppermute | solution.py:267
  31.9 25.3 %collective-permute-start.6 = (bf16[2,64,1536]{2,1,0:T(8,128)(2,1)S(1)}, bf16[2,64,1536]{2,1,0:T(8,128)(2,1)S(1)}, u32[]{:S(2)}, u32[]{:S(2)}) collective-permute-start(bf16[2,64,1536]{2,1,0:T(8,128)(2,1)S(1)} %pad_maximum_fusion), channel_id=1, source_target_pairs={{0,24},{8,32},{16,40},{24,48},{33,57},{41,1},{49,9},{57,17},{2,26}... | collective-permute-start | bytes 1179656 | tf_op jit(solution)/shard_map/ppermute | solution.py:267
  39.5 17.7 %collective-permute-start.7 = (bf16[2,64,1536]{2,1,0:T(8,128)(2,1)S(1)}, bf16[2,64,1536]{2,1,0:T(8,128)(2,1)S(1)}, u32[]{:S(2)}, u32[]{:S(2)}) collective-permute-start(bf16[2,64,1536]{2,1,0:T(8,128)(2,1)S(1)} %pad_maximum_fusion), channel_id=1, source_target_pairs={{0,56},{8,0},{16,8},{24,16},{33,25},{41,33},{49,41},{57,49},{2,58}... | collective-permute-start | bytes 1179656 | tf_op jit(solution)/shard_map/ppermute | solution.py:267
  66.1 10.5 %copy-start = (bf16[1024,1536]{1,0:T(8,128)(2,1)S(1)}, bf16[1024,1536]{1,0:T(8,128)(2,1)}, u32[]{:S(2)}) copy-start(bf16[1024,1536]{1,0:T(8,128)(2,1)} %own_ref.3) | copy-start | bytes 9437188
  66.1 112.8 %all-to-all-start.1 = ((bf16[8,4,2,128,256]{4,3,2,1,0:T(8,128)(2,1)}), bf16[8,4,2,128,256]{4,3,2,1,0:T(8,128)(2,1)}, u32[]{:S(2)}, u32[]{:S(2)}) async-start(bf16[8,4,2,128,256]{4,3,2,1,0:T(8,128)(2,1)} %copy.32), calls=%async_computation.1 | async-start | bytes 8388608 | tf_op jit(solution)/shard_map/all_to_all | solution.py:321
  76.5 28.1 %copy-start.10 = (s32[2,16]{1,0:T(2,128)S(1)}, s32[2,16]{1,0:T(2,128)}, u32[]{:S(2)}) copy-start(s32[2,16]{1,0:T(2,128)} %count_ref.1) | copy-start | bytes 388
  76.6 8.1 %collective-permute-start.8 = (bf16[1024,1536]{1,0:T(8,128)(2,1)S(1)}, bf16[1024,1536]{1,0:T(8,128)(2,1)S(1)}, u32[]{:S(2)}, u32[]{:S(2)}) collective-permute-start(bf16[1024,1536]{1,0:T(8,128)(2,1)S(1)} %copy-done), channel_id=1, source_target_pairs={{0,1},{1,0},{2,3},{3,2},{4,5},{5,4},{6,7},{7,6},{8,9},{9,8},{10,11... | collective-permute-start | bytes 9437192 | tf_op jit(solution)/shard_map/ppermute | solution.py:256
  81.1 21.0 %collective-permute-start.10 = (bf16[2,2,64,1536]{3,2,1,0:T(8,128)(2,1)}, bf16[2,2,64,1536]{3,2,1,0:T(8,128)(2,1)S(1)}, u32[]{:S(2)}, u32[]{:S(2)}) collective-permute-start(bf16[2,2,64,1536]{3,2,1,0:T(8,128)(2,1)} %get-tuple-element.40.rest_0_), channel_id=1, source_target_pairs={{0,128},{64,192},{128,0},{192,64},{1,129},{65,193},{129,1},{193,65... | collective-permute-start | bytes 2359304 | tf_op jit(solution)/shard_map/ppermute | solution.py:256
  82.0 36.1 %collective-permute-start.11 = (bf16[2,2,64,1536]{3,2,1,0:T(8,128)(2,1)}, bf16[2,2,64,1536]{3,2,1,0:T(8,128)(2,1)}, u32[]{:S(2)}, u32[]{:S(2)}) collective-permute-start(bf16[2,2,64,1536]{3,2,1,0:T(8,128)(2,1)} %get-tuple-element.40.rest_0_), channel_id=1, source_target_pairs={{0,192},{64,0},{128,64},{192,128},{1,193},{65,1},{129,65},{193,129... | collective-permute-start | bytes 2359304 | tf_op jit(solution)/shard_map/ppermute | solution.py:256
  84.0 35.3 %collective-permute-start.9 = (bf16[2,2,64,1536]{3,2,1,0:T(8,128)(2,1)}, bf16[2,2,64,1536]{3,2,1,0:T(8,128)(2,1)}, u32[]{:S(2)}, u32[]{:S(2)}) collective-permute-start(bf16[2,2,64,1536]{3,2,1,0:T(8,128)(2,1)} %get-tuple-element.40.rest_0_), channel_id=1, source_target_pairs={{0,64},{64,128},{128,192},{192,0},{1,65},{65,129},{129,193},{193,1... | collective-permute-start | bytes 2359304 | tf_op jit(solution)/shard_map/ppermute | solution.py:256
  84.0 52.4 %collective-permute-start.15 = (bf16[2,2,64,1536]{3,2,1,0:T(8,128)(2,1)}, bf16[2,2,64,1536]{3,2,1,0:T(8,128)(2,1)}, u32[]{:S(2)}, u32[]{:S(2)}) collective-permute-start(bf16[2,2,64,1536]{3,2,1,0:T(8,128)(2,1)} %get-tuple-element.30.rest_0_), channel_id=1, source_target_pairs={{0,64},{64,128},{128,192},{192,0},{1,65},{65,129},{129,193},{193,1... | collective-permute-start | bytes 2359304 | tf_op jit(solution)/shard_map/ppermute | solution.py:256
  84.7 1.7 copy-start.1
  86.4 66.3 %collective-permute-start.16 = (bf16[2,2,64,1536]{3,2,1,0:T(8,128)(2,1)}, bf16[2,2,64,1536]{3,2,1,0:T(8,128)(2,1)}, u32[]{:S(2)}, u32[]{:S(2)}) collective-permute-start(bf16[2,2,64,1536]{3,2,1,0:T(8,128)(2,1)} %get-tuple-element.30.rest_0_), channel_id=1, source_target_pairs={{0,128},{64,192},{128,0},{192,64},{1,129},{65,193},{129,1},{193,65... | collective-permute-start | bytes 2359304 | tf_op jit(solution)/shard_map/ppermute | solution.py:256
  102.1 0.9 copy-start.6
  103.0 49.7 %collective-permute-start.17 = (bf16[2,2,64,1536]{3,2,1,0:T(8,128)(2,1)}, bf16[2,2,64,1536]{3,2,1,0:T(8,128)(2,1)}, u32[]{:S(2)}, u32[]{:S(2)}) collective-permute-start(bf16[2,2,64,1536]{3,2,1,0:T(8,128)(2,1)} %get-tuple-element.30.rest_0_), channel_id=1, source_target_pairs={{0,192},{64,0},{128,64},{192,128},{1,193},{65,1},{129,65},{193,129... | collective-permute-start | bytes 2359304 | tf_op jit(solution)/shard_map/ppermute | solution.py:256
  119.2 1.9 copy-start.2
  121.1 1.1 copy-start.7
  129.3 0.7 copy-start.11
  130.0 0.7 copy-start.12
  130.7 34.3 %collective-permute-start.12 = (bf16[1024,128]{1,0:T(8,128)(2,1)}, bf16[1024,128]{1,0:T(8,128)(2,1)}, u32[]{:S(2)}, u32[]{:S(2)}) collective-permute-start(bf16[1024,128]{1,0:T(8,128)(2,1)} %get-tuple-element.27), channel_id=1, source_target_pairs={{0,2},{2,4},{4,6},{6,0},{1,3},{3,5},{5,7},{7,1},{8,10},{10,12},{12... | collective-permute-start | bytes 786440 | tf_op jit(solution)/shard_map/ppermute | solution.py:256
  132.3 34.6 %collective-permute-start.13 = (bf16[1024,128]{1,0:T(8,128)(2,1)}, bf16[1024,128]{1,0:T(8,128)(2,1)}, u32[]{:S(2)}, u32[]{:S(2)}) collective-permute-start(bf16[1024,128]{1,0:T(8,128)(2,1)} %copy-done.12), channel_id=1, source_target_pairs={{0,6},{2,0},{4,2},{6,4},{1,7},{3,1},{5,3},{7,5},{8,14},{10,8},{12,... | collective-permute-start | bytes 786440 | tf_op jit(solution)/shard_map/ppermute | solution.py:256
  136.3 30.6 %collective-permute-start.14 = (bf16[1024,128]{1,0:T(8,128)(2,1)}, bf16[1024,128]{1,0:T(8,128)(2,1)}, u32[]{:S(2)}, u32[]{:S(2)}) collective-permute-start(bf16[1024,128]{1,0:T(8,128)(2,1)} %copy-done.11), channel_id=1, source_target_pairs={{0,4},{2,6},{4,0},{6,2},{1,5},{3,7},{5,1},{7,3},{8,12},{10,14},{12... | collective-permute-start | bytes 786440 | tf_op jit(solution)/shard_map/ppermute | solution.py:256
  139.2 27.4 %copy-start.14 = (s32[2,16]{1,0:T(2,128)S(1)}, s32[2,16]{1,0:T(2,128)}, u32[]{:S(2)}) copy-start(s32[2,16]{1,0:T(2,128)} %param.15) | copy-start | bytes 388
  152.7 1.9 copy-start.3
  154.6 12.3 %copy-start.9 = (s32[2,16,32]{2,1,0:T(8,128)S(1)}, s32[2,16,32]{2,1,0:T(8,128)}, u32[]{:S(2)}) copy-start(s32[2,16,32]{2,1,0:T(8,128)} %param.16) | copy-start | bytes 12292
  161.5 0.7 copy-start.8
  162.2 8.7 %collective-permute-start.18 = (bf16[1024,128]{1,0:T(8,128)(2,1)}, bf16[1024,128]{1,0:T(8,128)(2,1)S(1)}, u32[]{:S(2)}, u32[]{:S(2)}) collective-permute-start(bf16[1024,128]{1,0:T(8,128)(2,1)} %get-tuple-element.32), channel_id=1, source_target_pairs={{0,2},{2,4},{4,6},{6,0},{1,3},{3,5},{5,7},{7,1},{8,10},{10,12},{12... | collective-permute-start | bytes 786440 | tf_op jit(solution)/shard_map/ppermute | solution.py:256
  163.5 7.4 %collective-permute-start.19 = (bf16[1024,128]{1,0:T(8,128)(2,1)}, bf16[1024,128]{1,0:T(8,128)(2,1)S(1)}, u32[]{:S(2)}, u32[]{:S(2)}) collective-permute-start(bf16[1024,128]{1,0:T(8,128)(2,1)} %get-tuple-element.33), channel_id=1, source_target_pairs={{0,6},{2,0},{4,2},{6,4},{1,7},{3,1},{5,3},{7,5},{8,14},{10,8},{12,... | collective-permute-start | bytes 786440 | tf_op jit(solution)/shard_map/ppermute | solution.py:256
  165.0 12.6 %collective-permute-start.20 = (bf16[1024,128]{1,0:T(8,128)(2,1)}, bf16[1024,128]{1,0:T(8,128)(2,1)S(1)}, u32[]{:S(2)}, u32[]{:S(2)}) collective-permute-start(bf16[1024,128]{1,0:T(8,128)(2,1)} %get-tuple-element.34), channel_id=1, source_target_pairs={{0,4},{2,6},{4,0},{6,2},{1,5},{3,7},{5,1},{7,3},{8,12},{10,14},{12... | collective-permute-start | bytes 786440 | tf_op jit(solution)/shard_map/ppermute | solution.py:256
  168.2 10.9 %copy-start.5 = (bf16[1024,768]{1,0:T(8,128)(2,1)S(1)}, bf16[1024,768]{1,0:T(8,128)(2,1)}, u32[]{:S(2)}) copy-start(bf16[1024,768]{1,0:T(8,128)(2,1)} %q_ref.1) | copy-start | bytes 4718596
  178.9 21.0 %copy-start.4 = (bf16[1024,256]{1,0:T(8,128)(2,1)}, bf16[1024,256]{1,0:T(8,128)(2,1)S(1)}, u32[]{:S(2)}) copy-start(bf16[1024,256]{1,0:T(8,128)(2,1)S(1)} %fusion.new_ref) | copy-start | bytes 1572868

commit v3 on v2

--- a/solution.py
+++ b/solution.py
@@ -115,6 +115,7 @@
     pos_row_ref,
     pos_lane_ref,
     arrived_ref,
+    token_ref,
     out_ref,
     raw,
     keys,
@@ -148,7 +149,6 @@
 
     def blend(r, k):
         c = span_ref[r, k]
-        copy(r, k).wait()
         pos = pos_row_ref[pl.ds(r * spans + c, 1), :]
         marked = (place == pos) & (slot < count_ref[r, c])
         first = pl.multiple_of(r * rows_request + c * per_span, per_span)
@@ -168,7 +168,6 @@
         length = (g + 1) * 2 * span_len
         stacked = []
         for k in (2 * g, 2 * g + 1):
-            blend(r, k)
             block = q_ref[pl.ds(first_row(r, k), per_span), :]
             stacked += [block[:, h * HEAD : (h + 1) * HEAD] for h in range(heads)]
         scores[step % 2, :, :length] = lax.dot_general(
@@ -212,6 +211,12 @@
                     used, mixed[at : at + per_span], 0.0
                 ).astype(BF16)
 
+    for r in range(requests):
+        for k in range(spans):
+            copy(r, k).wait()
+    for r in range(requests):
+        for k in range(spans):
+            blend(r, k)
     score(0)
     for step in range(len(groups)):
         if step + 1 < len(groups):
@@ -219,7 +224,7 @@
         attend(step)
 
 
-def attend(page_at, span_at, counts, queries, new_kv, positions, arrived):
+def attend(page_at, span_at, counts, queries, new_kv, positions, arrived, token):
     requests, spans = span_at.shape
     per_span = positions.shape[2]
     span_len = arrived.shape[1]
@@ -236,7 +241,7 @@
     return pl.pallas_call(
         functools.partial(attend_kernel, spans, per_span),
         out_shape=jax.ShapeDtypeStruct(queries.shape, BF16),
-        in_specs=[smem, smem, smem, vmem, vmem, vmem, vmem, pl.BlockSpec(memory_space=pl.ANY)],
+        in_specs=[smem] * 3 + [vmem] * 4 + [pl.BlockSpec(memory_space=pl.ANY)] * 2,
         out_specs=vmem,
         scratch_shapes=[
             pltpu.VMEM((requests, length, kv_width), BF16),
@@ -248,7 +253,7 @@
         ],
         compiler_params=pltpu.CompilerParams(vmem_limit_bytes=48 << 20),
         cost_estimate=pl.CostEstimate(flops=0, bytes_accessed=1024, transcendentals=0),
-    )(page_at, span_at, counts, queries, new_kv, pos_row, pos_lane, arrived)
+    )(page_at, span_at, counts, queries, new_kv, pos_row, pos_lane, arrived, token)
 
 
 def shift(x, axis, by):
@@ -271,13 +276,16 @@
     return gathered
 
 
-def new_rows(hidden, gathered):
+def new_rows(hidden, other, gathered):
     ahead = (lax.axis_index("x") - lax.axis_index("y") - jnp.arange(4)) % 4
-    other = shift(hidden, "core", 1)
-    parts = []
-    for part in range(2):
-        piece = gathered[2 * part : 2 * part + 2]
-        parts.append([piece] + [shift(piece, "x", by) for by in (1, 2, 3)])
+    keys, values = gathered[:2], gathered[2:]
+    keys_left, values_right = shift(keys, "x", 1), shift(values, "x", 3)
+    values_left, keys_right = shift(values, "x", 1), shift(keys, "x", 3)
+    keys_far, values_far = shift(keys_left, "x", 1), shift(values_right, "x", 3)
+    parts = [
+        [keys, keys_left, keys_far, keys_right],
+        [values, values_left, values_far, values_right],
+    ]
     totals = []
     for weights in parts:
         if totals:
@@ -314,14 +322,16 @@
     shard, outgoing = lax.optimization_barrier((kv_weight.T, outgoing))
     pair = jnp.stack([shard, shift(shard, "core", 1)])
     gathered = gather_over_z(pair)
+    other = shift(hidden, "core", 1)
+    gathered, other = lax.optimization_barrier((gathered, other))
     outgoing = outgoing.reshape(4, 8, 2, span_len, kv_width)
     halfway = lax.all_to_all(outgoing, "x", split_axis=0, concat_axis=0, tiled=True)
     halfway = halfway.transpose(1, 0, 2, 3, 4)
-    halfway, gathered = lax.optimization_barrier((halfway, gathered))
+    halfway, token = lax.optimization_barrier((halfway, gathered))
     arrived = lax.all_to_all(halfway, "z", split_axis=0, concat_axis=0, tiled=True)
     arrived = arrived.reshape(stores * 2, span_len, kv_width)
 
-    own_kv = new_rows(hidden, gathered)
+    own_kv = new_rows(hidden, other, gathered)
     row_used = jnp.arange(per_span)[None, None, :] < counts[:, :, None]
     new_kv = jnp.where(row_used.reshape(-1, 1), own_kv, 0.0).astype(BF16)
 
@@ -332,7 +342,7 @@
     at_rank = span_order[:, None, :] == jnp.arange(spans)[None, :, None]
     span_at = jnp.sum(at_rank * jnp.arange(spans)[None, None, :], axis=2)
     page_at = jnp.sum(at_rank * page_of[:, None, :], axis=2)
-    attended = attend(page_at, span_at, counts, queries, new_kv, positions, arrived)
+    attended = attend(page_at, span_at, counts, queries, new_kv, positions, arrived, token)
     return attended, new_kv
 
 

time: 201 us -> 190 us (0.945)
  waiting for transfers between devices: 83.4 us -> 97.7 us
  starting transfers between devices: 46.3 us -> 36.3 us
  local copies, waits for them, and re-layouts: 20.7 us -> 14.1 us
  Pallas kernels: 41 us -> 36.6 us
  other arithmetic: 7.26 us -> 3.34 us
    all_to_all x1, waiting for transfers between devices: 0.01 us -> 19.1 us  [body(): lax.all_to_all(halfway, 'z', split_axis=0, concat_axis=0, tiled=True)]
    ppermute x14, waiting for transfers between devices: 53.4 us -> 39.2 us  [shift(): return lax.ppermute(x, axis, [(i, (i + by) % size) for i in range(size)])]
    pallas_call x1, Pallas kernels: 20.8 us -> 12.9 us  [attend(): pl.pallas_call(functools.partial(attend_kernel, spans, per_span), out_sha...]
    all_to_all x1, waiting for transfers between devices: 3.38 us -> 10.3 us  [body(): lax.all_to_all(outgoing, 'x', split_axis=0, concat_axis=0, tiled=True)]
    ppermute x14, starting transfers between devices: 23.6 us -> 17.6 us  [shift(): return lax.ppermute(x, axis, [(i, (i + by) % size) for i in range(size)])]
    all_to_all x1, starting transfers between devices: 10.5 us -> 6.5 us  [body(): lax.all_to_all(halfway, 'z', split_axis=0, concat_axis=0, tiled=True)]
    pallas_call x2, Pallas kernels: 14 us -> 17.9 us  [project(): pl.pallas_call(project_kernel, out_shape=[jax.ShapeDtypeStruct((rows, blo...]
    unnamed x32 -> x22, local copies, waits for them, and re-layouts: 11.2 us -> 8.18 us
  transfers between devices with their start and end apart: 23 -> 23, of which waited for: 13 -> 13; matrix products, arithmetic and copies ran while one was open for 5% -> 3% of each run, Pallas kernels for 7% -> 13%
where the time goes in v3:
time: 190 us; the launch traced here: 189 us
  waiting for transfers between devices  97.7 us (51%)
  Pallas kernels  36.6 us (19%)
  starting transfers between devices  36.3 us (19%)
  local copies, waits for them, and re-layouts  14.1 us (7%)
  other arithmetic  3.34 us (2%)
    ppermute x14, waiting for transfers between devices, shift(): return lax.ppermute(x, axis, [(i, (i + by) % size) for i in range(size)])  39.2 us
    ppermute x7, waiting for transfers between devices, gather_over_z(): near.append(lax.ppermute(pair, ('z', 'core'), moves) if hop else pair)  29.1 us
    all_to_all x1, waiting for transfers between devices, body(): lax.all_to_all(halfway, 'z', split_axis=0, concat_axis=0, tiled=True)  19.1 us
    pallas_call x2, Pallas kernels, project(): pl.pallas_call(project_kernel, out_shape=[jax.ShapeDtypeStruct((rows, blo...  17.9 us
    ppermute x14, starting transfers between devices, shift(): return lax.ppermute(x, axis, [(i, (i + by) % size) for i in range(size)])  17.6 us
    pallas_call x1, Pallas kernels, attend(): pl.pallas_call(functools.partial(attend_kernel, spans, per_span), out_sha...  12.9 us
    all_to_all x1, waiting for transfers between devices, body(): lax.all_to_all(outgoing, 'x', split_axis=0, concat_axis=0, tiled=True)  10.3 us
    unnamed x22, local copies, waits for them, and re-layouts  8.18 us
  transfers between devices with their start and end apart: 23, of which 13 were waited for; matrix products, arithmetic and copies ran while one was open for 3% of the time, Pallas kernels for 13%

profile of v3, /device:TPU:1, one launch (start us, length us, event | category | flops | bytes accessed | tf_op | source)
XLA Modules:
  0.0 189.3 jit_solution(5010006593019976650)
XLA Ops:
  0.6 3.3 %collective-permute-start.8 = (bf16[1024,1536]{1,0:T(8,128)(2,1)}, bf16[1024,1536]{1,0:T(8,128)(2,1)}, u32[]{:S(2)}, u32[]{:S(2)}) collective-permute-start(bf16[1024,1536]{1,0:T(8,128)(2,1)} %own_ref.3), channel_id=1, source_target_pairs={{0,1},{1,0},{2,3},{3,2},{4,5},{5,4},{6,7},{7,6},{8,9},{9,8},{10,11... | collective-permute-start | bytes 9437192 | tf_op jit(solution)/shard_map/ppermute | solution.py:261
  4.0 0.8 copy.28
  4.7 0.8 copy.30
  6.3 0.5 and_select_fusion.1.slot_ref
  6.8 5.8 %shard_map.104 = bf16[64,128,256]{2,1,0:T(8,128)(2,1)} custom-call(s32[64]{0:T(128)} %and_select_fusion.1.slot_ref, bf16[32,128,256]{2,1,0:T(8,128)(2,1)} %pages_ref.1), custom_call_target="tpu_custom_call" | custom-call | bytes 1024 | tf_op jit(solution)/shard_map/pallas_call | solution.py:40
  12.7 5.0 %all-to-all-start = ((bf16[4,8,2,128,256]{4,3,2,1,0:T(8,128)(2,1)}), bf16[4,8,2,128,256]{4,3,2,1,0:T(8,128)(2,1)}, u32[]{:S(2)}, u32[]{:S(2)}) async-start(bf16[4,8,2,128,256]{4,3,2,1,0:T(8,128)(2,1)} %bitcast.21), calls=%async_computation | async-start | bytes 8388608 | tf_op jit(solution)/shard_map/all_to_all | solution.py:328
  17.8 1.4 collective-permute-done
  19.3 1.3 collective-permute-start.1
  20.8 1.3 collective-permute-start.2
  22.1 0.7 collective-permute-start.3
  22.8 1.3 collective-permute-start.4
  24.1 7.9 %collective-permute-done.1 = bf16[2,64,1536]{2,1,0:T(8,128)(2,1)S(1)} collective-permute-done((bf16[2,64,1536]{2,1,0:T(8,128)(2,1)S(1)}, bf16[2,64,1536]{2,1,0:T(8,128)(2,1)S(1)}, u32[]{:S(2)}, u32[]{:S(2)}) %collective-permute-start.1) | collective-permute-done | bytes 393248 | tf_op jit(solution)/shard_map/ppermute | solution.py:272
  31.9 0.7 collective-permute-start.5
  32.8 7.3 %collective-permute-done.2 = bf16[2,64,1536]{2,1,0:T(8,128)(2,1)S(1)} collective-permute-done((bf16[2,64,1536]{2,1,0:T(8,128)(2,1)S(1)}, bf16[2,64,1536]{2,1,0:T(8,128)(2,1)S(1)}, u32[]{:S(2)}, u32[]{:S(2)}) %collective-permute-start.2) | collective-permute-done | bytes 393248 | tf_op jit(solution)/shard_map/ppermute | solution.py:272
  40.2 1.3 collective-permute-start.6
  41.5 0.7 collective-permute-start.7
  42.3 2.1 %collective-permute-done.4 = bf16[2,64,1536]{2,1,0:T(8,128)(2,1)S(1)} collective-permute-done((bf16[2,64,1536]{2,1,0:T(8,128)(2,1)S(1)}, bf16[2,64,1536]{2,1,0:T(8,128)(2,1)S(1)}, u32[]{:S(2)}, u32[]{:S(2)}) %collective-permute-start.4) | collective-permute-done | bytes 393248 | tf_op jit(solution)/shard_map/ppermute | solution.py:272
  44.5 11.8 %collective-permute-done.6 = bf16[2,64,1536]{2,1,0:T(8,128)(2,1)S(1)} collective-permute-done((bf16[2,64,1536]{2,1,0:T(8,128)(2,1)S(1)}, bf16[2,64,1536]{2,1,0:T(8,128)(2,1)S(1)}, u32[]{:S(2)}, u32[]{:S(2)}) %collective-permute-start.6) | collective-permute-done | bytes 393248 | tf_op jit(solution)/shard_map/ppermute | solution.py:272
  56.4 10.3 %all-to-all-done = bf16[4,8,2,128,256]{4,3,2,1,0:T(8,128)(2,1)} async-done(((bf16[4,8,2,128,256]{4,3,2,1,0:T(8,128)(2,1)}), bf16[4,8,2,128,256]{4,3,2,1,0:T(8,128)(2,1)}, u32[]{:S(2)}, u32[]{:S(2)}) %all-to-all-start) | async-done | bytes 4194336 | tf_op jit(solution)/shard_map/all_to_all | solution.py:328
  66.7 4.6 %copy.32 = bf16[8,4,2,128,256]{4,3,2,1,0:T(8,128)(2,1)} copy(bf16[8,4,2,128,256]{4,3,2,0,1:T(8,128)(2,1)} %bitcast.13) | data formatting | bytes 8388608 | tf_op jit(solution)/shard_map/optimization_barrier | solution.py:330
  71.3 6.5 %all-to-all-start.1 = ((bf16[8,4,2,128,256]{4,3,2,1,0:T(8,128)(2,1)}), bf16[8,4,2,128,256]{4,3,2,1,0:T(8,128)(2,1)}, u32[]{:S(2)}, u32[]{:S(2)}) async-start(bf16[8,4,2,128,256]{4,3,2,1,0:T(8,128)(2,1)} %copy.32), calls=%async_computation.1 | async-start | bytes 8388608 | tf_op jit(solution)/shard_map/all_to_all | solution.py:331
  77.9 0.4 collective-permute-start.9
  78.3 2.4 %collective-permute-start.16 = (bf16[2,2,64,1536]{3,2,1,0:T(8,128)(2,1)S(1)}, bf16[2,2,64,1536]{3,2,1,0:T(8,128)(2,1)}, u32[]{:S(2)}, u32[]{:S(2)}) collective-permute-start(bf16[2,2,64,1536]{3,2,1,0:T(8,128)(2,1)S(1)} %get-tuple-element.32.rest_0_), channel_id=1, source_target_pairs={{0,192},{64,0},{128,64},{192,128},{1,193},{65,1},{129,65},{193,129... | collective-permute-start | bytes 2359304 | tf_op jit(solution)/shard_map/ppermute | solution.py:261
  80.7 16.5 %collective-permute-done.9.rest_1_ = bf16[2,2,64,1536]{3,2,1,0:T(8,128)(2,1)} collective-permute-done((bf16[2,2,64,1536]{3,2,1,0:T(8,128)(2,1)S(1)}, bf16[2,2,64,1536]{3,2,1,0:T(8,128)(2,1)}, u32[]{:S(2)}, u32[]{:S(2)}) %collective-permute-start.9) | collective-permute-done | bytes 786464 | tf_op jit(solution)/shard_map/ppermute | solution.py:261
  97.3 2.7 %collective-permute-start.17 = (bf16[2,2,64,1536]{3,2,1,0:T(8,128)(2,1)}, bf16[2,2,64,1536]{3,2,1,0:T(8,128)(2,1)}, u32[]{:S(2)}, u32[]{:S(2)}) collective-permute-start(bf16[2,2,64,1536]{3,2,1,0:T(8,128)(2,1)} %collective-permute-done.16.rest_3_), channel_id=1, source_target_pairs={{0,192},{64,0},{128,64},{192,128},{1,193},{65,1},{129,65},{193,129... | collective-permute-start | bytes 2359304 | tf_op jit(solution)/shard_map/ppermute | solution.py:261
  100.2 12.8 %collective-permute-done.11.rest_3_ = bf16[2,2,64,1536]{3,2,1,0:T(8,128)(2,1)} collective-permute-done((bf16[2,2,64,1536]{3,2,1,0:T(8,128)(2,1)S(1)}, bf16[2,2,64,1536]{3,2,1,0:T(8,128)(2,1)}, u32[]{:S(2)}, u32[]{:S(2)}) %collective-permute-start.11) | collective-permute-done | bytes 786464 | tf_op jit(solution)/shard_map/ppermute | solution.py:261
  113.0 2.8 %collective-permute-done.10.rest_2_ = bf16[2,2,64,1536]{3,2,1,0:T(8,128)(2,1)} collective-permute-done((bf16[2,2,64,1536]{3,2,1,0:T(8,128)(2,1)}, bf16[2,2,64,1536]{3,2,1,0:T(8,128)(2,1)}, u32[]{:S(2)}, u32[]{:S(2)}) %collective-permute-start.10) | collective-permute-done | bytes 786464 | tf_op jit(solution)/shard_map/ppermute | solution.py:261
  115.8 1.9 copy-done
  117.7 8.9 %shard_map.105 = (bf16[1024,128]{1,0:T(8,128)(2,1)S(1)}, bf16[1024,128]{1,0:T(8,128)(2,1)}, bf16[1024,128]{1,0:T(8,128)(2,1)S(1)}, bf16[1024,128]{1,0:T(8,128)(2,1)S(1)}) custom-call(s32[4]{0:T(128)S(1)} %and_select_fusion.slot_ref, bf16[1024,1536]{1,0:T(8,128)(2,1)S(1)} %copy-done, bf16[1024,1536]{1,0:T(8,128)(2,1)} %collective-permute-done.8.other_ref, ...), custom_call_target="tpu_custom_call" | custom-call | bytes 1024 | tf_op jit(solution)/shard_map/pallas_call | solution.py:93
  126.6 0.7 copy-done.6
  127.3 0.7 copy-done.7
  128.0 1.3 collective-permute-start.12
  129.7 1.6 collective-permute-start.13
  131.3 1.6 collective-permute-start.14
  133.0 1.9 copy-done.1
  134.8 9.0 %shard_map.106 = (bf16[1024,128]{1,0:T(8,128)(2,1)S(1)}, bf16[1024,128]{1,0:T(8,128)(2,1)}, bf16[1024,128]{1,0:T(8,128)(2,1)S(1)}, bf16[1024,128]{1,0:T(8,128)(2,1)}) custom-call(s32[4]{0:T(128)S(1)} %and_select_fusion.slot_ref, bf16[1024,1536]{1,0:T(8,128)(2,1)S(1)} %copy-done.1, bf16[1024,1536]{1,0:T(8,128)(2,1)} %collective-permute-done.8.other_ref, ...), custom_call_target="tpu_custom_call" | custom-call | bytes 1024 | tf_op jit(solution)/shard_map/pallas_call | solution.py:93
  143.8 1.1 collective-permute-start.18
  144.9 1.7 collective-permute-start.19
  146.6 1.4 collective-permute-start.20
  148.3 1.3 convert_add_fusion.1
  149.6 1.1 collective-permute-done.18
  150.7 2.4 %collective-permute-done.19 = bf16[1024,128]{1,0:T(8,128)(2,1)S(1)} collective-permute-done((bf16[1024,128]{1,0:T(8,128)(2,1)}, bf16[1024,128]{1,0:T(8,128)(2,1)S(1)}, u32[]{:S(2)}, u32[]{:S(2)}) %collective-permute-start.19) | collective-permute-done | bytes 262176 | tf_op jit(solution)/shard_map/ppermute | solution.py:261
  153.1 2.1 %collective-permute-done.20 = bf16[1024,128]{1,0:T(8,128)(2,1)S(1)} collective-permute-done((bf16[1024,128]{1,0:T(8,128)(2,1)S(1)}, bf16[1024,128]{1,0:T(8,128)(2,1)S(1)}, u32[]{:S(2)}, u32[]{:S(2)}) %collective-permute-start.20) | collective-permute-done | bytes 262176 | tf_op jit(solution)/shard_map/ppermute | solution.py:261
  155.3 0.2 fusion.new_ref
  155.5 19.1 %all-to-all-done.1 = bf16[8,4,2,128,256]{4,3,2,1,0:T(8,128)(2,1)} async-done(((bf16[8,4,2,128,256]{4,3,2,1,0:T(8,128)(2,1)}), bf16[8,4,2,128,256]{4,3,2,1,0:T(8,128)(2,1)}, u32[]{:S(2)}, u32[]{:S(2)}) %all-to-all-start.1) | async-done | bytes 4194336 | tf_op jit(solution)/shard_map/all_to_all | solution.py:331
  174.7 0.2 broadcast_in_dim.61.pos_lane_ref
  174.9 1.4 copy-done.3
  176.3 12.9 %shard_map.107 = bf16[1024,768]{1,0:T(8,128)(2,1)} custom-call(s32[2,16]{1,0:T(2,128)S(1)} %get-tuple-element.43.page_ref, s32[2,16]{1,0:T(2,128)S(1)} %get-tuple-element.42.span_ref, s32[2,16]{1,0:T(2,128)S(1)} %copy-done.5, bf16[1024,768]{1,0:T(8,128)(2,1)S(1)} %copy-done.3, bf16[1024,256]{1,0:T(8,128)(2,1)S(1)} %fusion.new_ref, s32[32,32]{1,0:T(8,128)S(1)} %bitcast.20, ...), custom_call_target="tpu_custom_call" | custom-call | bytes 1024 | tf_op jit(solution)/shard_map/pallas_call | solution.py:241
  (59 shorter events, 2.6 us)
Async XLA Ops:
  0.6 55.7 %collective-permute-start.8 = (bf16[1024,1536]{1,0:T(8,128)(2,1)}, bf16[1024,1536]{1,0:T(8,128)(2,1)}, u32[]{:S(2)}, u32[]{:S(2)}) collective-permute-start(bf16[1024,1536]{1,0:T(8,128)(2,1)} %own_ref.3), channel_id=1, source_target_pairs={{0,1},{1,0},{2,3},{3,2},{4,5},{5,4},{6,7},{7,6},{8,9},{9,8},{10,11... | collective-permute-start | bytes 9437192 | tf_op jit(solution)/shard_map/ppermute | solution.py:261
  12.7 5.0 %copy-start.8 = (bf16[1536,64]{0,1:T(8,128)(2,1)S(1)}, bf16[1536,64]{0,1:T(8,128)(2,1)}, u32[]{:S(2)}) copy-start(bf16[1536,64]{0,1:T(8,128)(2,1)} %param.10) | copy-start | bytes 589828
  12.7 54.0 %all-to-all-start = ((bf16[4,8,2,128,256]{4,3,2,1,0:T(8,128)(2,1)}), bf16[4,8,2,128,256]{4,3,2,1,0:T(8,128)(2,1)}, u32[]{:S(2)}, u32[]{:S(2)}) async-start(bf16[4,8,2,128,256]{4,3,2,1,0:T(8,128)(2,1)} %bitcast.21), calls=%async_computation | async-start | bytes 8388608 | tf_op jit(solution)/shard_map/all_to_all | solution.py:328
  17.7 1.5 collective-permute-start
  19.3 12.7 %collective-permute-start.1 = (bf16[2,64,1536]{2,1,0:T(8,128)(2,1)S(1)}, bf16[2,64,1536]{2,1,0:T(8,128)(2,1)S(1)}, u32[]{:S(2)}, u32[]{:S(2)}) collective-permute-start(bf16[2,64,1536]{2,1,0:T(8,128)(2,1)S(1)} %pad_maximum_fusion), channel_id=1, source_target_pairs={{0,32},{8,40},{16,48},{24,56},{33,1},{41,9},{49,17},{57,25},{2,34}... | collective-permute-start | bytes 1179656 | tf_op jit(solution)/shard_map/ppermute | solution.py:272
  20.8 19.4 %collective-permute-start.2 = (bf16[2,64,1536]{2,1,0:T(8,128)(2,1)S(1)}, bf16[2,64,1536]{2,1,0:T(8,128)(2,1)S(1)}, u32[]{:S(2)}, u32[]{:S(2)}) collective-permute-start(bf16[2,64,1536]{2,1,0:T(8,128)(2,1)S(1)} %pad_maximum_fusion), channel_id=1, source_target_pairs={{0,8},{8,16},{16,24},{24,32},{33,41},{41,49},{49,57},{57,1},{2,10}... | collective-permute-start | bytes 1179656 | tf_op jit(solution)/shard_map/ppermute | solution.py:272
  22.1 19.4 %collective-permute-start.3 = (bf16[2,64,1536]{2,1,0:T(8,128)(2,1)S(1)}, bf16[2,64,1536]{2,1,0:T(8,128)(2,1)S(1)}, u32[]{:S(2)}, u32[]{:S(2)}) collective-permute-start(bf16[2,64,1536]{2,1,0:T(8,128)(2,1)S(1)} %pad_maximum_fusion), channel_id=1, source_target_pairs={{0,40},{8,48},{16,56},{24,0},{33,9},{41,17},{49,25},{57,33},{2,42}... | collective-permute-start | bytes 1179656 | tf_op jit(solution)/shard_map/ppermute | solution.py:272
  22.8 21.6 %collective-permute-start.4 = (bf16[2,64,1536]{2,1,0:T(8,128)(2,1)S(1)}, bf16[2,64,1536]{2,1,0:T(8,128)(2,1)S(1)}, u32[]{:S(2)}, u32[]{:S(2)}) collective-permute-start(bf16[2,64,1536]{2,1,0:T(8,128)(2,1)S(1)} %pad_maximum_fusion), channel_id=1, source_target_pairs={{0,16},{8,24},{16,32},{24,40},{33,49},{41,57},{49,1},{57,9},{2,18}... | collective-permute-start | bytes 1179656 | tf_op jit(solution)/shard_map/ppermute | solution.py:272
  31.9 12.4 %collective-permute-start.5 = (bf16[2,64,1536]{2,1,0:T(8,128)(2,1)S(1)}, bf16[2,64,1536]{2,1,0:T(8,128)(2,1)S(1)}, u32[]{:S(2)}, u32[]{:S(2)}) collective-permute-start(bf16[2,64,1536]{2,1,0:T(8,128)(2,1)S(1)} %pad_maximum_fusion), channel_id=1, source_target_pairs={{0,48},{8,56},{16,0},{24,8},{33,17},{41,25},{49,33},{57,41},{2,50}... | collective-permute-start | bytes 1179656 | tf_op jit(solution)/shard_map/ppermute | solution.py:272
  40.2 16.1 %collective-permute-start.6 = (bf16[2,64,1536]{2,1,0:T(8,128)(2,1)S(1)}, bf16[2,64,1536]{2,1,0:T(8,128)(2,1)S(1)}, u32[]{:S(2)}, u32[]{:S(2)}) collective-permute-start(bf16[2,64,1536]{2,1,0:T(8,128)(2,1)S(1)} %pad_maximum_fusion), channel_id=1, source_target_pairs={{0,24},{8,32},{16,40},{24,48},{33,57},{41,1},{49,9},{57,17},{2,26}... | collective-permute-start | bytes 1179656 | tf_op jit(solution)/shard_map/ppermute | solution.py:272
  41.5 14.8 %collective-permute-start.7 = (bf16[2,64,1536]{2,1,0:T(8,128)(2,1)S(1)}, bf16[2,64,1536]{2,1,0:T(8,128)(2,1)S(1)}, u32[]{:S(2)}, u32[]{:S(2)}) collective-permute-start(bf16[2,64,1536]{2,1,0:T(8,128)(2,1)S(1)} %pad_maximum_fusion), channel_id=1, source_target_pairs={{0,56},{8,0},{16,8},{24,16},{33,25},{41,33},{49,41},{57,49},{2,58}... | collective-permute-start | bytes 1179656 | tf_op jit(solution)/shard_map/ppermute | solution.py:272
  71.3 103.3 %all-to-all-start.1 = ((bf16[8,4,2,128,256]{4,3,2,1,0:T(8,128)(2,1)}), bf16[8,4,2,128,256]{4,3,2,1,0:T(8,128)(2,1)}, u32[]{:S(2)}, u32[]{:S(2)}) async-start(bf16[8,4,2,128,256]{4,3,2,1,0:T(8,128)(2,1)} %copy.32), calls=%async_computation.1 | async-start | bytes 8388608 | tf_op jit(solution)/shard_map/all_to_all | solution.py:331
  77.8 22.3 %copy-start.5 = (s32[2,16]{1,0:T(2,128)S(1)}, s32[2,16]{1,0:T(2,128)}, u32[]{:S(2)}) copy-start(s32[2,16]{1,0:T(2,128)} %count_ref.1) | copy-start | bytes 388
  77.9 19.3 %collective-permute-start.9 = (bf16[2,2,64,1536]{3,2,1,0:T(8,128)(2,1)S(1)}, bf16[2,2,64,1536]{3,2,1,0:T(8,128)(2,1)}, u32[]{:S(2)}, u32[]{:S(2)}) collective-permute-start(bf16[2,2,64,1536]{3,2,1,0:T(8,128)(2,1)S(1)} %get-tuple-element.44.rest_0_), channel_id=1, source_target_pairs={{0,64},{64,128},{128,192},{192,0},{1,65},{65,129},{129,193},{193,1... | collective-permute-start | bytes 2359304 | tf_op jit(solution)/shard_map/ppermute | solution.py:261
  78.3 19.0 %collective-permute-start.16 = (bf16[2,2,64,1536]{3,2,1,0:T(8,128)(2,1)S(1)}, bf16[2,2,64,1536]{3,2,1,0:T(8,128)(2,1)}, u32[]{:S(2)}, u32[]{:S(2)}) collective-permute-start(bf16[2,2,64,1536]{3,2,1,0:T(8,128)(2,1)S(1)} %get-tuple-element.32.rest_0_), channel_id=1, source_target_pairs={{0,192},{64,0},{128,64},{192,128},{1,193},{65,1},{129,65},{193,129... | collective-permute-start | bytes 2359304 | tf_op jit(solution)/shard_map/ppermute | solution.py:261
  80.7 32.3 %collective-permute-start.11 = (bf16[2,2,64,1536]{3,2,1,0:T(8,128)(2,1)S(1)}, bf16[2,2,64,1536]{3,2,1,0:T(8,128)(2,1)}, u32[]{:S(2)}, u32[]{:S(2)}) collective-permute-start(bf16[2,2,64,1536]{3,2,1,0:T(8,128)(2,1)S(1)} %get-tuple-element.44.rest_0_), channel_id=1, source_target_pairs={{0,192},{64,0},{128,64},{192,128},{1,193},{65,1},{129,65},{193,129... | collective-permute-start | bytes 2359304 | tf_op jit(solution)/shard_map/ppermute | solution.py:261
  97.3 18.5 %collective-permute-start.10 = (bf16[2,2,64,1536]{3,2,1,0:T(8,128)(2,1)}, bf16[2,2,64,1536]{3,2,1,0:T(8,128)(2,1)}, u32[]{:S(2)}, u32[]{:S(2)}) collective-permute-start(bf16[2,2,64,1536]{3,2,1,0:T(8,128)(2,1)} %collective-permute-done.9.rest_1_), channel_id=1, source_target_pairs={{0,64},{64,128},{128,192},{192,0},{1,65},{65,129},{129,193},{193,1... | collective-permute-start | bytes 2359304 | tf_op jit(solution)/shard_map/ppermute | solution.py:261
  97.3 35.7 %collective-permute-start.15 = (bf16[2,2,64,1536]{3,2,1,0:T(8,128)(2,1)S(1)}, bf16[2,2,64,1536]{3,2,1,0:T(8,128)(2,1)}, u32[]{:S(2)}, u32[]{:S(2)}) collective-permute-start(bf16[2,2,64,1536]{3,2,1,0:T(8,128)(2,1)S(1)} %get-tuple-element.32.rest_0_), channel_id=1, source_target_pairs={{0,64},{64,128},{128,192},{192,0},{1,65},{65,129},{129,193},{193,1... | collective-permute-start | bytes 2359304 | tf_op jit(solution)/shard_map/ppermute | solution.py:261
  97.3 35.7 %collective-permute-start.17 = (bf16[2,2,64,1536]{3,2,1,0:T(8,128)(2,1)}, bf16[2,2,64,1536]{3,2,1,0:T(8,128)(2,1)}, u32[]{:S(2)}, u32[]{:S(2)}) collective-permute-start(bf16[2,2,64,1536]{3,2,1,0:T(8,128)(2,1)} %collective-permute-done.16.rest_3_), channel_id=1, source_target_pairs={{0,192},{64,0},{128,64},{192,128},{1,193},{65,1},{129,65},{193,129... | collective-permute-start | bytes 2359304 | tf_op jit(solution)/shard_map/ppermute | solution.py:261
  115.8 1.9 copy-start
  126.6 0.7 copy-start.6
  127.3 0.7 copy-start.7
  128.0 18.6 %collective-permute-start.12 = (bf16[1024,128]{1,0:T(8,128)(2,1)}, bf16[1024,128]{1,0:T(8,128)(2,1)}, u32[]{:S(2)}, u32[]{:S(2)}) collective-permute-start(bf16[1024,128]{1,0:T(8,128)(2,1)} %get-tuple-element.29), channel_id=1, source_target_pairs={{0,2},{2,4},{4,6},{6,0},{1,3},{3,5},{5,7},{7,1},{8,10},{10,12},{12... | collective-permute-start | bytes 786440 | tf_op jit(solution)/shard_map/ppermute | solution.py:261
  129.7 18.6 %collective-permute-start.13 = (bf16[1024,128]{1,0:T(8,128)(2,1)}, bf16[1024,128]{1,0:T(8,128)(2,1)}, u32[]{:S(2)}, u32[]{:S(2)}) collective-permute-start(bf16[1024,128]{1,0:T(8,128)(2,1)} %copy-done.7), channel_id=1, source_target_pairs={{0,6},{2,0},{4,2},{6,4},{1,7},{3,1},{5,3},{7,5},{8,14},{10,8},{12,... | collective-permute-start | bytes 786440 | tf_op jit(solution)/shard_map/ppermute | solution.py:261
  131.3 17.1 %collective-permute-start.14 = (bf16[1024,128]{1,0:T(8,128)(2,1)}, bf16[1024,128]{1,0:T(8,128)(2,1)}, u32[]{:S(2)}, u32[]{:S(2)}) collective-permute-start(bf16[1024,128]{1,0:T(8,128)(2,1)} %copy-done.6), channel_id=1, source_target_pairs={{0,4},{2,6},{4,0},{6,2},{1,5},{3,7},{5,1},{7,3},{8,12},{10,14},{12... | collective-permute-start | bytes 786440 | tf_op jit(solution)/shard_map/ppermute | solution.py:261
  132.9 15.1 %copy-start.9 = (s32[2,16]{1,0:T(2,128)S(1)}, s32[2,16]{1,0:T(2,128)}, u32[]{:S(2)}) copy-start(s32[2,16]{1,0:T(2,128)} %param.15) | copy-start | bytes 388
  132.9 1.9 copy-start.1
  134.8 13.4 %copy-start.4 = (s32[2,16,32]{2,1,0:T(8,128)S(1)}, s32[2,16,32]{2,1,0:T(8,128)}, u32[]{:S(2)}) copy-start(s32[2,16,32]{2,1,0:T(8,128)} %param.16) | copy-start | bytes 12292
  143.8 6.8 %collective-permute-start.18 = (bf16[1024,128]{1,0:T(8,128)(2,1)}, bf16[1024,128]{1,0:T(8,128)(2,1)S(1)}, u32[]{:S(2)}, u32[]{:S(2)}) collective-permute-start(bf16[1024,128]{1,0:T(8,128)(2,1)} %get-tuple-element.34), channel_id=1, source_target_pairs={{0,2},{2,4},{4,6},{6,0},{1,3},{3,5},{5,7},{7,1},{8,10},{10,12},{12... | collective-permute-start | bytes 786440 | tf_op jit(solution)/shard_map/ppermute | solution.py:261
  144.9 8.1 %collective-permute-start.19 = (bf16[1024,128]{1,0:T(8,128)(2,1)}, bf16[1024,128]{1,0:T(8,128)(2,1)S(1)}, u32[]{:S(2)}, u32[]{:S(2)}) collective-permute-start(bf16[1024,128]{1,0:T(8,128)(2,1)} %get-tuple-element.35), channel_id=1, source_target_pairs={{0,6},{2,0},{4,2},{6,4},{1,7},{3,1},{5,3},{7,5},{8,14},{10,8},{12,... | collective-permute-start | bytes 786440 | tf_op jit(solution)/shard_map/ppermute | solution.py:261
  146.6 8.6 %collective-permute-start.20 = (bf16[1024,128]{1,0:T(8,128)(2,1)S(1)}, bf16[1024,128]{1,0:T(8,128)(2,1)S(1)}, u32[]{:S(2)}, u32[]{:S(2)}) collective-permute-start(bf16[1024,128]{1,0:T(8,128)(2,1)S(1)} %get-tuple-element.36), channel_id=1, source_target_pairs={{0,4},{2,6},{4,0},{6,2},{1,5},{3,7},{5,1},{7,3},{8,12},{10,14},{12... | collective-permute-start | bytes 786440 | tf_op jit(solution)/shard_map/ppermute | solution.py:261
  155.5 33.6 %copy-start.2 = (bf16[1024,256]{1,0:T(8,128)(2,1)}, bf16[1024,256]{1,0:T(8,128)(2,1)S(1)}, u32[]{:S(2)}) copy-start(bf16[1024,256]{1,0:T(8,128)(2,1)S(1)} %fusion.new_ref) | copy-start | bytes 1572868
  174.9 1.4 copy-start.3

commit v4 on v3

--- a/solution.py
+++ b/solution.py
@@ -310,14 +310,15 @@
     entries = requests * spans
     span_len, kv_width = pages.shape[1:]
 
-    owners = page_owner.reshape(stores, entries)
-    slots = page_slot.reshape(stores, entries)
-    entry = jnp.arange(entries)[None, :]
-    mine = owners == store_index
-    code = entry * pages.shape[0] + slots
-    first = jnp.min(jnp.where(mine, code, entries * pages.shape[0]), axis=1)
+    depth = pages.shape[0]
+    row = jnp.arange(page_owner.shape[0])[:, None] % requests
+    mine = page_owner == store_index
+    code = (row * spans + jnp.arange(spans)[None, :]) * depth + page_slot
+    first = jnp.min(jnp.where(mine, code, entries * depth), axis=1)
     last = jnp.max(jnp.where(mine, code, 0), axis=1)
-    source_slot = jnp.stack([first, last], axis=1).reshape(-1) % pages.shape[0]
+    first = jnp.min(first.reshape(stores, requests), axis=1)
+    last = jnp.max(last.reshape(stores, requests), axis=1)
+    source_slot = jnp.stack([first, last], axis=1).reshape(-1) % depth
     outgoing = pack_pages(source_slot, pages)
     shard, outgoing = lax.optimization_barrier((kv_weight.T, outgoing))
     pair = jnp.stack([shard, shift(shard, "core", 1)])
@@ -335,14 +336,15 @@
     row_used = jnp.arange(per_span)[None, None, :] < counts[:, :, None]
     new_kv = jnp.where(row_used.reshape(-1, 1), own_kv, 0.0).astype(BF16)
 
-    my_owner = lax.dynamic_index_in_dim(owners, store_index, 0, keepdims=False)
+    my_owner = lax.dynamic_slice_in_dim(page_owner, store_index * requests, requests, 0)
+    my_owner = my_owner.reshape(entries)
     earlier = jnp.arange(entries)[None, :] < jnp.arange(entries)[:, None]
     second = jnp.any((my_owner[:, None] == my_owner[None, :]) & earlier, axis=1)
     page_of = ((my_owner % 8 * 4 + my_owner // 8) * 2 + second.astype(jnp.int32)).reshape(requests, spans)
     at_rank = span_order[:, None, :] == jnp.arange(spans)[None, :, None]
     span_at = jnp.sum(at_rank * jnp.arange(spans)[None, None, :], axis=2)
     page_at = jnp.sum(at_rank * page_of[:, None, :], axis=2)
-    attended = attend(page_at, span_at, counts, queries, new_kv, positions, arrived, token)
+    attended = attend(page_at, span_at, counts, queries, new_kv, positions, arrived, token[0, 0, :16, :HEAD])
     return attended, new_kv
 
 

time: 190 us -> 188 us (0.989)
  other arithmetic: 3.34 us -> 8.66 us
  Pallas kernels: 36.6 us -> 31.8 us
  waiting for transfers between devices: 97.7 us -> 94.3 us
    ppermute x7, waiting for transfers between devices: 29.1 us -> 23.5 us  [gather_over_z(): near.append(lax.ppermute(pair, ('z', 'core'), moves) if hop else pair)]
    pallas_call x2, Pallas kernels: 17.9 us -> 13 us  [project(): pl.pallas_call(project_kernel, out_shape=[jax.ShapeDtypeStruct((rows, blo...]
    unnamed x22 -> x23, local copies, waits for them, and re-layouts: 8.18 us -> 3.91 us
    dynamic_update_slice x4, other arithmetic: 0.39 us -> 4.35 us  [gather_over_z(): lax.dynamic_update_slice(gathered, piece[None], ((z - by) % 4, 0, 0, 0))]
    ppermute x14, waiting for transfers between devices: 39.2 us -> 43 us  [shift(): return lax.ppermute(x, axis, [(i, (i + by) % size) for i in range(size)])]
    slice x1, local copies, waits for them, and re-layouts: 0.1 us -> 2.78 us  [new_rows(): keys, values = (gathered[:2], gathered[2:])]
  transfers between devices with their start and end apart: 23 -> 23, of which waited for: 13 -> 13; matrix products, arithmetic and copies ran while one was open for 3% -> 8% of each run, Pallas kernels for 13% -> 10%
where the time goes in v4:
time: 188 us
  waiting for transfers between devices  94.3 us (50%)
  starting transfers between devices  37.2 us (20%)
  Pallas kernels  31.8 us (17%)
  local copies, waits for them, and re-layouts  14.3 us (8%)
  other arithmetic  8.66 us (5%)
    ppermute x14, waiting for transfers between devices, shift(): return lax.ppermute(x, axis, [(i, (i + by) % size) for i in range(size)])  43 us
    ppermute x7, waiting for transfers between devices, gather_over_z(): near.append(lax.ppermute(pair, ('z', 'core'), moves) if hop else pair)  23.5 us
    ppermute x14, starting transfers between devices, shift(): return lax.ppermute(x, axis, [(i, (i + by) % size) for i in range(size)])  18.1 us
    all_to_all x1, waiting for transfers between devices, body(): lax.all_to_all(halfway, 'z', split_axis=0, concat_axis=0, tiled=True)  17.8 us
    pallas_call x2, Pallas kernels, project(): pl.pallas_call(project_kernel, out_shape=[jax.ShapeDtypeStruct((rows, blo...  13 us
    pallas_call x1, Pallas kernels, attend(): pl.pallas_call(functools.partial(attend_kernel, spans, per_span), out_sha...  12.9 us
    all_to_all x1, waiting for transfers between devices, body(): lax.all_to_all(outgoing, 'x', split_axis=0, concat_axis=0, tiled=True)  10.1 us
    ppermute x7, starting transfers between devices, gather_over_z(): near.append(lax.ppermute(pair, ('z', 'core'), moves) if hop else pair)  7.19 us
  transfers between devices with their start and end apart: 23, of which 13 were waited for; matrix products, arithmetic and copies ran while one was open for 8% of the time, Pallas kernels for 10%

profile of v4, /device:TPU:1, one launch (start us, length us, event | category | flops | bytes accessed | tf_op | source)
XLA Modules:
  0.0 187.5 jit_solution(4348519276565299084)
XLA Ops:
  0.6 3.3 %collective-permute-start.8 = (bf16[1024,1536]{1,0:T(8,128)(2,1)}, bf16[1024,1536]{1,0:T(8,128)(2,1)S(1)}, u32[]{:S(2)}, u32[]{:S(2)}) collective-permute-start(bf16[1024,1536]{1,0:T(8,128)(2,1)} %own_ref.3), channel_id=1, source_target_pairs={{0,1},{1,0},{2,3},{3,2},{4,5},{5,4},{6,7},{7,6},{8,9},{9,8},{10,11... | collective-permute-start | bytes 9437192 | tf_op jit(solution)/shard_map/ppermute | solution.py:261
  4.0 0.7 select_reduce_fusion.3
  5.4 0.5 and_select_fusion.1.slot_ref
  5.9 5.9 %shard_map.104 = bf16[64,128,256]{2,1,0:T(8,128)(2,1)} custom-call(s32[64]{0:T(128)} %and_select_fusion.1.slot_ref, bf16[32,128,256]{2,1,0:T(8,128)(2,1)} %pages_ref.1), custom_call_target="tpu_custom_call" | custom-call | bytes 1024 | tf_op jit(solution)/shard_map/pallas_call | solution.py:40
  11.8 5.0 %all-to-all-start = ((bf16[4,8,2,128,256]{4,3,2,1,0:T(8,128)(2,1)}), bf16[4,8,2,128,256]{4,3,2,1,0:T(8,128)(2,1)}, u32[]{:S(2)}, u32[]{:S(2)}) async-start(bf16[4,8,2,128,256]{4,3,2,1,0:T(8,128)(2,1)} %bitcast.20), calls=%async_computation | async-start | bytes 8388608 | tf_op jit(solution)/shard_map/all_to_all | solution.py:329
  17.0 1.4 collective-permute-done
  18.4 0.8 pad_maximum_fusion
  19.1 1.3 collective-permute-start.1
  20.6 1.3 collective-permute-start.2
  21.9 0.7 collective-permute-start.3
  22.6 1.3 collective-permute-start.4
  23.9 8.1 %collective-permute-done.1 = bf16[2,64,1536]{2,1,0:T(8,128)(2,1)} collective-permute-done((bf16[2,64,1536]{2,1,0:T(8,128)(2,1)}, bf16[2,64,1536]{2,1,0:T(8,128)(2,1)}, u32[]{:S(2)}, u32[]{:S(2)}) %collective-permute-start.1) | collective-permute-done | bytes 393248 | tf_op jit(solution)/shard_map/ppermute | solution.py:272
  32.1 0.7 collective-permute-start.5
  32.8 1.3 broadcast_in_dim.51
  34.0 1.8 bitcast_dynamic-update-slice_fusion.3
  35.9 4.7 %collective-permute-done.2 = bf16[2,64,1536]{2,1,0:T(8,128)(2,1)S(1)} collective-permute-done((bf16[2,64,1536]{2,1,0:T(8,128)(2,1)}, bf16[2,64,1536]{2,1,0:T(8,128)(2,1)S(1)}, u32[]{:S(2)}, u32[]{:S(2)}) %collective-permute-start.2) | collective-permute-done | bytes 393248 | tf_op jit(solution)/shard_map/ppermute | solution.py:272
  40.6 1.3 collective-permute-start.6
  41.9 0.7 collective-permute-start.7
  42.6 0.8 bitcast_dynamic-update-slice_fusion.2
  43.4 10.6 %collective-permute-done.4 = bf16[2,64,1536]{2,1,0:T(8,128)(2,1)S(1)} collective-permute-done((bf16[2,64,1536]{2,1,0:T(8,128)(2,1)}, bf16[2,64,1536]{2,1,0:T(8,128)(2,1)S(1)}, u32[]{:S(2)}, u32[]{:S(2)}) %collective-permute-start.4) | collective-permute-done | bytes 393248 | tf_op jit(solution)/shard_map/ppermute | solution.py:272
  54.0 0.8 bitcast_dynamic-update-slice_fusion.1
  54.9 0.8 bitcast_dynamic-update-slice_fusion
  55.7 10.1 %all-to-all-done = bf16[4,8,2,128,256]{4,3,2,1,0:T(8,128)(2,1)} async-done(((bf16[4,8,2,128,256]{4,3,2,1,0:T(8,128)(2,1)}), bf16[4,8,2,128,256]{4,3,2,1,0:T(8,128)(2,1)}, u32[]{:S(2)}, u32[]{:S(2)}) %all-to-all-start) | async-done | bytes 4194336 | tf_op jit(solution)/shard_map/all_to_all | solution.py:329
  65.8 4.6 %copy.25 = bf16[8,4,2,128,256]{4,3,2,1,0:T(8,128)(2,1)} copy(bf16[8,4,2,128,256]{4,3,2,0,1:T(8,128)(2,1)} %bitcast.11) | data formatting | bytes 8388608 | tf_op jit(solution)/shard_map/optimization_barrier | solution.py:331
  70.4 7.0 %all-to-all-start.1 = ((bf16[8,4,2,128,256]{4,3,2,1,0:T(8,128)(2,1)}), bf16[8,4,2,128,256]{4,3,2,1,0:T(8,128)(2,1)}, u32[]{:S(2)}, u32[]{:S(2)}) async-start(bf16[8,4,2,128,256]{4,3,2,1,0:T(8,128)(2,1)} %copy.25), calls=%async_computation.1 | async-start | bytes 8388608 | tf_op jit(solution)/shard_map/all_to_all | solution.py:332
  77.4 2.8 %fusion.8 = (bf16[2,2,64,1536]{3,2,1,0:T(8,128)(2,1)}, bf16[2,2,64,1536]{3,2,1,0:T(8,128)(2,1)}) fusion(bf16[4,2,64,1536]{3,2,1,0:T(8,128)(2,1)} %bitcast_dynamic-update-slice_fusion), kind=kLoop, calls=%fused_computation.41 | loop fusion | bytes 3145728 | tf_op jit(solution)/shard_map/slice | solution.py:281
  80.5 2.4 %collective-permute-start.16 = (bf16[2,2,64,1536]{3,2,1,0:T(8,128)(2,1)}, bf16[2,2,64,1536]{3,2,1,0:T(8,128)(2,1)}, u32[]{:S(2)}, u32[]{:S(2)}) collective-permute-start(bf16[2,2,64,1536]{3,2,1,0:T(8,128)(2,1)} %get-tuple-element.32.rest_0_), channel_id=1, source_target_pairs={{0,192},{64,0},{128,64},{192,128},{1,193},{65,1},{129,65},{193,129... | collective-permute-start | bytes 2359304 | tf_op jit(solution)/shard_map/ppermute | solution.py:261
  82.9 16.7 %collective-permute-done.9.rest_1_ = bf16[2,2,64,1536]{3,2,1,0:T(8,128)(2,1)} collective-permute-done((bf16[2,2,64,1536]{3,2,1,0:T(8,128)(2,1)}, bf16[2,2,64,1536]{3,2,1,0:T(8,128)(2,1)}, u32[]{:S(2)}, u32[]{:S(2)}) %collective-permute-start.9) | collective-permute-done | bytes 786464 | tf_op jit(solution)/shard_map/ppermute | solution.py:261
  99.9 2.7 %collective-permute-start.17 = (bf16[2,2,64,1536]{3,2,1,0:T(8,128)(2,1)}, bf16[2,2,64,1536]{3,2,1,0:T(8,128)(2,1)}, u32[]{:S(2)}, u32[]{:S(2)}) collective-permute-start(bf16[2,2,64,1536]{3,2,1,0:T(8,128)(2,1)} %collective-permute-done.16.rest_3_), channel_id=1, source_target_pairs={{0,192},{64,0},{128,64},{192,128},{1,193},{65,1},{129,65},{193,129... | collective-permute-start | bytes 2359304 | tf_op jit(solution)/shard_map/ppermute | solution.py:261
  103.0 12.5 %collective-permute-done.11.rest_3_ = bf16[2,2,64,1536]{3,2,1,0:T(8,128)(2,1)} collective-permute-done((bf16[2,2,64,1536]{3,2,1,0:T(8,128)(2,1)}, bf16[2,2,64,1536]{3,2,1,0:T(8,128)(2,1)}, u32[]{:S(2)}, u32[]{:S(2)}) %collective-permute-start.11) | collective-permute-done | bytes 786464 | tf_op jit(solution)/shard_map/ppermute | solution.py:261
  115.5 2.7 %collective-permute-done.10.rest_2_ = bf16[2,2,64,1536]{3,2,1,0:T(8,128)(2,1)} collective-permute-done((bf16[2,2,64,1536]{3,2,1,0:T(8,128)(2,1)}, bf16[2,2,64,1536]{3,2,1,0:T(8,128)(2,1)}, u32[]{:S(2)}, u32[]{:S(2)}) %collective-permute-start.10) | collective-permute-done | bytes 786464 | tf_op jit(solution)/shard_map/ppermute | solution.py:261
  118.2 1.9 %copy-done.2 = bf16[1024,1536]{1,0:T(8,128)(2,1)S(1)} copy-done((bf16[1024,1536]{1,0:T(8,128)(2,1)S(1)}, bf16[1024,1536]{1,0:T(8,128)(2,1)}, u32[]{:S(2)}) %copy-start.2) | copy-done | bytes 3145752
  120.1 6.9 %shard_map.105 = (bf16[1024,128]{1,0:T(8,128)(2,1)S(1)}, bf16[1024,128]{1,0:T(8,128)(2,1)}, bf16[1024,128]{1,0:T(8,128)(2,1)}, bf16[1024,128]{1,0:T(8,128)(2,1)}) custom-call(s32[4]{0:T(128)S(1)} %and_select_fusion.slot_ref, bf16[1024,1536]{1,0:T(8,128)(2,1)S(1)} %copy-done, bf16[1024,1536]{1,0:T(8,128)(2,1)S(1)} %copy-done.2, ...), custom_call_target="tpu_custom_call" | custom-call | bytes 1024 | tf_op jit(solution)/shard_map/pallas_call | solution.py:93
  127.0 1.4 collective-permute-start.12
  128.4 1.7 collective-permute-start.13
  130.1 1.6 collective-permute-start.14
  132.1 3.0 %collective-permute-done.15.rest_1_ = bf16[2,2,64,1536]{3,2,1,0:T(8,128)(2,1)} collective-permute-done((bf16[2,2,64,1536]{3,2,1,0:T(8,128)(2,1)}, bf16[2,2,64,1536]{3,2,1,0:T(8,128)(2,1)}, u32[]{:S(2)}, u32[]{:S(2)}) %collective-permute-start.15) | collective-permute-done | bytes 786464 | tf_op jit(solution)/shard_map/ppermute | solution.py:261
  135.1 1.9 %copy-done.3 = bf16[1024,1536]{1,0:T(8,128)(2,1)S(1)} copy-done((bf16[1024,1536]{1,0:T(8,128)(2,1)S(1)}, bf16[1024,1536]{1,0:T(8,128)(2,1)}, u32[]{:S(2)}) %copy-start.3) | copy-done | bytes 3145752
  137.0 6.1 %shard_map.106 = (bf16[1024,128]{1,0:T(8,128)(2,1)S(1)}, bf16[1024,128]{1,0:T(8,128)(2,1)S(1)}, bf16[1024,128]{1,0:T(8,128)(2,1)S(1)}, bf16[1024,128]{1,0:T(8,128)(2,1)S(1)}) custom-call(s32[4]{0:T(128)S(1)} %and_select_fusion.slot_ref, bf16[1024,1536]{1,0:T(8,128)(2,1)S(1)} %copy-done, bf16[1024,1536]{1,0:T(8,128)(2,1)S(1)} %copy-done.3, ...), custom_call_target="tpu_custom_call" | custom-call | bytes 1024 | tf_op jit(solution)/shard_map/pallas_call | solution.py:93
  143.0 1.4 collective-permute-start.18
  144.4 1.5 collective-permute-start.19
  145.9 1.6 collective-permute-start.20
  147.5 0.7 slice_bitcast_fusion.token_ref
  148.2 1.2 convert_add_fusion.1
  149.4 0.6 collective-permute-done.18
  150.4 5.8 %collective-permute-done.20 = bf16[1024,128]{1,0:T(8,128)(2,1)S(1)} collective-permute-done((bf16[1024,128]{1,0:T(8,128)(2,1)S(1)}, bf16[1024,128]{1,0:T(8,128)(2,1)S(1)}, u32[]{:S(2)}, u32[]{:S(2)}) %collective-permute-start.20) | collective-permute-done | bytes 262176 | tf_op jit(solution)/shard_map/ppermute | solution.py:261
  156.5 17.8 %all-to-all-done.1 = bf16[8,4,2,128,256]{4,3,2,1,0:T(8,128)(2,1)} async-done(((bf16[8,4,2,128,256]{4,3,2,1,0:T(8,128)(2,1)}), bf16[8,4,2,128,256]{4,3,2,1,0:T(8,128)(2,1)}, u32[]{:S(2)}, u32[]{:S(2)}) %all-to-all-start.1) | async-done | bytes 4194336 | tf_op jit(solution)/shard_map/all_to_all | solution.py:332
  174.5 12.9 %shard_map.107 = bf16[1024,768]{1,0:T(8,128)(2,1)} custom-call(s32[2,16]{1,0:T(2,128)S(1)} %get-tuple-element.43.page_ref, s32[2,16]{1,0:T(2,128)S(1)} %get-tuple-element.42.span_ref, s32[2,16]{1,0:T(2,128)S(1)} %copy-done.7, bf16[1024,768]{1,0:T(8,128)(2,1)S(1)} %copy-done.5, bf16[1024,256]{1,0:T(8,128)(2,1)S(1)} %fusion.new_ref, s32[32,32]{1,0:T(8,128)S(1)} %bitcast.19, ...), custom_call_target="tpu_custom_call" | custom-call | bytes 1024 | tf_op jit(solution)/shard_map/pallas_call | solution.py:241
  (59 shorter events, 3.0 us)
Async XLA Ops:
  0.6 55.1 %collective-permute-start.8 = (bf16[1024,1536]{1,0:T(8,128)(2,1)}, bf16[1024,1536]{1,0:T(8,128)(2,1)S(1)}, u32[]{:S(2)}, u32[]{:S(2)}) collective-permute-start(bf16[1024,1536]{1,0:T(8,128)(2,1)} %own_ref.3), channel_id=1, source_target_pairs={{0,1},{1,0},{2,3},{3,2},{4,5},{5,4},{6,7},{7,6},{8,9},{9,8},{10,11... | collective-permute-start | bytes 9437192 | tf_op jit(solution)/shard_map/ppermute | solution.py:261
  11.8 5.0 %copy-start.8 = (bf16[1536,64]{0,1:T(8,128)(2,1)S(1)}, bf16[1536,64]{0,1:T(8,128)(2,1)}, u32[]{:S(2)}) copy-start(bf16[1536,64]{0,1:T(8,128)(2,1)} %param.10) | copy-start | bytes 589828
  11.8 54.0 %all-to-all-start = ((bf16[4,8,2,128,256]{4,3,2,1,0:T(8,128)(2,1)}), bf16[4,8,2,128,256]{4,3,2,1,0:T(8,128)(2,1)}, u32[]{:S(2)}, u32[]{:S(2)}) async-start(bf16[4,8,2,128,256]{4,3,2,1,0:T(8,128)(2,1)} %bitcast.20), calls=%async_computation | async-start | bytes 8388608 | tf_op jit(solution)/shard_map/all_to_all | solution.py:329
  16.8 1.5 collective-permute-start
  19.1 12.9 %collective-permute-start.1 = (bf16[2,64,1536]{2,1,0:T(8,128)(2,1)}, bf16[2,64,1536]{2,1,0:T(8,128)(2,1)}, u32[]{:S(2)}, u32[]{:S(2)}) collective-permute-start(bf16[2,64,1536]{2,1,0:T(8,128)(2,1)} %pad_maximum_fusion), channel_id=1, source_target_pairs={{0,32},{8,40},{16,48},{24,56},{33,1},{41,9},{49,17},{57,25},{2,34}... | collective-permute-start | bytes 1179656 | tf_op jit(solution)/shard_map/ppermute | solution.py:272
  20.6 20.0 %collective-permute-start.2 = (bf16[2,64,1536]{2,1,0:T(8,128)(2,1)}, bf16[2,64,1536]{2,1,0:T(8,128)(2,1)S(1)}, u32[]{:S(2)}, u32[]{:S(2)}) collective-permute-start(bf16[2,64,1536]{2,1,0:T(8,128)(2,1)} %pad_maximum_fusion), channel_id=1, source_target_pairs={{0,8},{8,16},{16,24},{24,32},{33,41},{41,49},{49,57},{57,1},{2,10}... | collective-permute-start | bytes 1179656 | tf_op jit(solution)/shard_map/ppermute | solution.py:272
  21.9 20.0 %collective-permute-start.3 = (bf16[2,64,1536]{2,1,0:T(8,128)(2,1)}, bf16[2,64,1536]{2,1,0:T(8,128)(2,1)S(1)}, u32[]{:S(2)}, u32[]{:S(2)}) collective-permute-start(bf16[2,64,1536]{2,1,0:T(8,128)(2,1)} %pad_maximum_fusion), channel_id=1, source_target_pairs={{0,40},{8,48},{16,56},{24,0},{33,9},{41,17},{49,25},{57,33},{2,42}... | collective-permute-start | bytes 1179656 | tf_op jit(solution)/shard_map/ppermute | solution.py:272
  22.6 31.4 %collective-permute-start.4 = (bf16[2,64,1536]{2,1,0:T(8,128)(2,1)}, bf16[2,64,1536]{2,1,0:T(8,128)(2,1)S(1)}, u32[]{:S(2)}, u32[]{:S(2)}) collective-permute-start(bf16[2,64,1536]{2,1,0:T(8,128)(2,1)} %pad_maximum_fusion), channel_id=1, source_target_pairs={{0,16},{8,24},{16,32},{24,40},{33,49},{41,57},{49,1},{57,9},{2,18}... | collective-permute-start | bytes 1179656 | tf_op jit(solution)/shard_map/ppermute | solution.py:272
  32.1 21.9 %collective-permute-start.5 = (bf16[2,64,1536]{2,1,0:T(8,128)(2,1)}, bf16[2,64,1536]{2,1,0:T(8,128)(2,1)S(1)}, u32[]{:S(2)}, u32[]{:S(2)}) collective-permute-start(bf16[2,64,1536]{2,1,0:T(8,128)(2,1)} %pad_maximum_fusion), channel_id=1, source_target_pairs={{0,48},{8,56},{16,0},{24,8},{33,17},{41,25},{49,33},{57,41},{2,50}... | collective-permute-start | bytes 1179656 | tf_op jit(solution)/shard_map/ppermute | solution.py:272
  40.6 14.3 %collective-permute-start.6 = (bf16[2,64,1536]{2,1,0:T(8,128)(2,1)}, bf16[2,64,1536]{2,1,0:T(8,128)(2,1)S(1)}, u32[]{:S(2)}, u32[]{:S(2)}) collective-permute-start(bf16[2,64,1536]{2,1,0:T(8,128)(2,1)} %pad_maximum_fusion), channel_id=1, source_target_pairs={{0,24},{8,32},{16,40},{24,48},{33,57},{41,1},{49,9},{57,17},{2,26}... | collective-permute-start | bytes 1179656 | tf_op jit(solution)/shard_map/ppermute | solution.py:272
  41.9 13.0 %collective-permute-start.7 = (bf16[2,64,1536]{2,1,0:T(8,128)(2,1)}, bf16[2,64,1536]{2,1,0:T(8,128)(2,1)S(1)}, u32[]{:S(2)}, u32[]{:S(2)}) collective-permute-start(bf16[2,64,1536]{2,1,0:T(8,128)(2,1)} %pad_maximum_fusion), channel_id=1, source_target_pairs={{0,56},{8,0},{16,8},{24,16},{33,25},{41,33},{49,41},{57,49},{2,58}... | collective-permute-start | bytes 1179656 | tf_op jit(solution)/shard_map/ppermute | solution.py:272
  55.7 14.7 %copy-start.1 = (bf16[1024,1536]{1,0:T(8,128)(2,1)}, bf16[1024,1536]{1,0:T(8,128)(2,1)S(1)}, u32[]{:S(2)}) copy-start(bf16[1024,1536]{1,0:T(8,128)(2,1)S(1)} %collective-permute-done.8.other_ref) | copy-start | bytes 9437188
  70.4 103.8 %all-to-all-start.1 = ((bf16[8,4,2,128,256]{4,3,2,1,0:T(8,128)(2,1)}), bf16[8,4,2,128,256]{4,3,2,1,0:T(8,128)(2,1)}, u32[]{:S(2)}, u32[]{:S(2)}) async-start(bf16[8,4,2,128,256]{4,3,2,1,0:T(8,128)(2,1)} %copy.25), calls=%async_computation.1 | async-start | bytes 8388608 | tf_op jit(solution)/shard_map/all_to_all | solution.py:332
  77.4 22.3 %copy-start.9 = (s32[64,16]{0,1:T(8,128)S(1)}, s32[64,16]{0,1:T(8,128)}, u32[]{:S(2)}) copy-start(s32[64,16]{0,1:T(8,128)} %param.13) | copy-start | bytes 12292
  77.4 25.5 %copy-start.7 = (s32[2,16]{1,0:T(2,128)S(1)}, s32[2,16]{1,0:T(2,128)}, u32[]{:S(2)}) copy-start(s32[2,16]{1,0:T(2,128)} %count_ref.1) | copy-start | bytes 388
  77.4 40.8 %copy-start = (bf16[1024,1536]{1,0:T(8,128)(2,1)S(1)}, bf16[1024,1536]{1,0:T(8,128)(2,1)}, u32[]{:S(2)}) copy-start(bf16[1024,1536]{1,0:T(8,128)(2,1)} %own_ref.3) | copy-start | bytes 9437188
  80.2 19.5 %collective-permute-start.9 = (bf16[2,2,64,1536]{3,2,1,0:T(8,128)(2,1)}, bf16[2,2,64,1536]{3,2,1,0:T(8,128)(2,1)}, u32[]{:S(2)}, u32[]{:S(2)}) collective-permute-start(bf16[2,2,64,1536]{3,2,1,0:T(8,128)(2,1)} %get-tuple-element.44.rest_0_), channel_id=1, source_target_pairs={{0,64},{64,128},{128,192},{192,0},{1,65},{65,129},{129,193},{193,1... | collective-permute-start | bytes 2359304 | tf_op jit(solution)/shard_map/ppermute | solution.py:261
  80.5 19.4 %collective-permute-start.16 = (bf16[2,2,64,1536]{3,2,1,0:T(8,128)(2,1)}, bf16[2,2,64,1536]{3,2,1,0:T(8,128)(2,1)}, u32[]{:S(2)}, u32[]{:S(2)}) collective-permute-start(bf16[2,2,64,1536]{3,2,1,0:T(8,128)(2,1)} %get-tuple-element.32.rest_0_), channel_id=1, source_target_pairs={{0,192},{64,0},{128,64},{192,128},{1,193},{65,1},{129,65},{193,129... | collective-permute-start | bytes 2359304 | tf_op jit(solution)/shard_map/ppermute | solution.py:261
  82.9 32.6 %collective-permute-start.11 = (bf16[2,2,64,1536]{3,2,1,0:T(8,128)(2,1)}, bf16[2,2,64,1536]{3,2,1,0:T(8,128)(2,1)}, u32[]{:S(2)}, u32[]{:S(2)}) collective-permute-start(bf16[2,2,64,1536]{3,2,1,0:T(8,128)(2,1)} %get-tuple-element.44.rest_0_), channel_id=1, source_target_pairs={{0,192},{64,0},{128,64},{192,128},{1,193},{65,1},{129,65},{193,129... | collective-permute-start | bytes 2359304 | tf_op jit(solution)/shard_map/ppermute | solution.py:261
  99.7 18.5 %collective-permute-start.10 = (bf16[2,2,64,1536]{3,2,1,0:T(8,128)(2,1)}, bf16[2,2,64,1536]{3,2,1,0:T(8,128)(2,1)}, u32[]{:S(2)}, u32[]{:S(2)}) collective-permute-start(bf16[2,2,64,1536]{3,2,1,0:T(8,128)(2,1)} %collective-permute-done.9.rest_1_), channel_id=1, source_target_pairs={{0,64},{64,128},{128,192},{192,0},{1,65},{65,129},{129,193},{193,1... | collective-permute-start | bytes 2359304 | tf_op jit(solution)/shard_map/ppermute | solution.py:261
  99.9 35.1 %collective-permute-start.15 = (bf16[2,2,64,1536]{3,2,1,0:T(8,128)(2,1)}, bf16[2,2,64,1536]{3,2,1,0:T(8,128)(2,1)}, u32[]{:S(2)}, u32[]{:S(2)}) collective-permute-start(bf16[2,2,64,1536]{3,2,1,0:T(8,128)(2,1)} %get-tuple-element.32.rest_0_), channel_id=1, source_target_pairs={{0,64},{64,128},{128,192},{192,0},{1,65},{65,129},{129,193},{193,1... | collective-permute-start | bytes 2359304 | tf_op jit(solution)/shard_map/ppermute | solution.py:261
  99.9 35.1 %collective-permute-start.17 = (bf16[2,2,64,1536]{3,2,1,0:T(8,128)(2,1)}, bf16[2,2,64,1536]{3,2,1,0:T(8,128)(2,1)}, u32[]{:S(2)}, u32[]{:S(2)}) collective-permute-start(bf16[2,2,64,1536]{3,2,1,0:T(8,128)(2,1)} %collective-permute-done.16.rest_3_), channel_id=1, source_target_pairs={{0,192},{64,0},{128,64},{192,128},{1,193},{65,1},{129,65},{193,129... | collective-permute-start | bytes 2359304 | tf_op jit(solution)/shard_map/ppermute | solution.py:261
  103.0 28.8 %copy-start.10 = (s32[2,16]{1,0:T(2,128)S(1)}, s32[2,16]{1,0:T(2,128)}, u32[]{:S(2)}) copy-start(s32[2,16]{1,0:T(2,128)} %param.15) | copy-start | bytes 388
  118.2 1.9 %copy-start.2 = (bf16[1024,1536]{1,0:T(8,128)(2,1)S(1)}, bf16[1024,1536]{1,0:T(8,128)(2,1)}, u32[]{:S(2)}) copy-start(bf16[1024,1536]{1,0:T(8,128)(2,1)} %copy-done.1) | copy-start | bytes 9437188
  120.1 11.9 %copy-start.6 = (s32[2,16,32]{2,1,0:T(8,128)S(1)}, s32[2,16,32]{2,1,0:T(8,128)}, u32[]{:S(2)}) copy-start(s32[2,16,32]{2,1,0:T(8,128)} %param.16) | copy-start | bytes 12292
  127.0 18.9 %collective-permute-start.12 = (bf16[1024,128]{1,0:T(8,128)(2,1)}, bf16[1024,128]{1,0:T(8,128)(2,1)}, u32[]{:S(2)}, u32[]{:S(2)}) collective-permute-start(bf16[1024,128]{1,0:T(8,128)(2,1)} %get-tuple-element.29), channel_id=1, source_target_pairs={{0,2},{2,4},{4,6},{6,0},{1,3},{3,5},{5,7},{7,1},{8,10},{10,12},{12... | collective-permute-start | bytes 786440 | tf_op jit(solution)/shard_map/ppermute | solution.py:261
  128.4 19.8 %collective-permute-start.13 = (bf16[1024,128]{1,0:T(8,128)(2,1)}, bf16[1024,128]{1,0:T(8,128)(2,1)}, u32[]{:S(2)}, u32[]{:S(2)}) collective-permute-start(bf16[1024,128]{1,0:T(8,128)(2,1)} %get-tuple-element.30), channel_id=1, source_target_pairs={{0,6},{2,0},{4,2},{6,4},{1,7},{3,1},{5,3},{7,5},{8,14},{10,8},{12,... | collective-permute-start | bytes 786440 | tf_op jit(solution)/shard_map/ppermute | solution.py:261
  130.1 18.0 %collective-permute-start.14 = (bf16[1024,128]{1,0:T(8,128)(2,1)}, bf16[1024,128]{1,0:T(8,128)(2,1)}, u32[]{:S(2)}, u32[]{:S(2)}) collective-permute-start(bf16[1024,128]{1,0:T(8,128)(2,1)} %get-tuple-element.31), channel_id=1, source_target_pairs={{0,4},{2,6},{4,0},{6,2},{1,5},{3,7},{5,1},{7,3},{8,12},{10,14},{12... | collective-permute-start | bytes 786440 | tf_op jit(solution)/shard_map/ppermute | solution.py:261
  135.1 1.9 %copy-start.3 = (bf16[1024,1536]{1,0:T(8,128)(2,1)S(1)}, bf16[1024,1536]{1,0:T(8,128)(2,1)}, u32[]{:S(2)}) copy-start(bf16[1024,1536]{1,0:T(8,128)(2,1)} %copy-done.1) | copy-start | bytes 9437188
  143.0 7.0 %collective-permute-start.18 = (bf16[1024,128]{1,0:T(8,128)(2,1)S(1)}, bf16[1024,128]{1,0:T(8,128)(2,1)S(1)}, u32[]{:S(2)}, u32[]{:S(2)}) collective-permute-start(bf16[1024,128]{1,0:T(8,128)(2,1)S(1)} %get-tuple-element.34), channel_id=1, source_target_pairs={{0,2},{2,4},{4,6},{6,0},{1,3},{3,5},{5,7},{7,1},{8,10},{10,12},{12... | collective-permute-start | bytes 786440 | tf_op jit(solution)/shard_map/ppermute | solution.py:261
  144.4 6.0 %collective-permute-start.19 = (bf16[1024,128]{1,0:T(8,128)(2,1)S(1)}, bf16[1024,128]{1,0:T(8,128)(2,1)S(1)}, u32[]{:S(2)}, u32[]{:S(2)}) collective-permute-start(bf16[1024,128]{1,0:T(8,128)(2,1)S(1)} %get-tuple-element.35), channel_id=1, source_target_pairs={{0,6},{2,0},{4,2},{6,4},{1,7},{3,1},{5,3},{7,5},{8,14},{10,8},{12,... | collective-permute-start | bytes 786440 | tf_op jit(solution)/shard_map/ppermute | solution.py:261
  145.9 10.2 %collective-permute-start.20 = (bf16[1024,128]{1,0:T(8,128)(2,1)S(1)}, bf16[1024,128]{1,0:T(8,128)(2,1)S(1)}, u32[]{:S(2)}, u32[]{:S(2)}) collective-permute-start(bf16[1024,128]{1,0:T(8,128)(2,1)S(1)} %get-tuple-element.36), channel_id=1, source_target_pairs={{0,4},{2,6},{4,0},{6,2},{1,5},{3,7},{5,1},{7,3},{8,12},{10,14},{12... | collective-permute-start | bytes 786440 | tf_op jit(solution)/shard_map/ppermute | solution.py:261
  149.4 25.0 %copy-start.5 = (bf16[1024,768]{1,0:T(8,128)(2,1)S(1)}, bf16[1024,768]{1,0:T(8,128)(2,1)}, u32[]{:S(2)}) copy-start(bf16[1024,768]{1,0:T(8,128)(2,1)} %q_ref.1) | copy-start | bytes 4718596
  156.5 30.9 %copy-start.4 = (bf16[1024,256]{1,0:T(8,128)(2,1)}, bf16[1024,256]{1,0:T(8,128)(2,1)S(1)}, u32[]{:S(2)}) copy-start(bf16[1024,256]{1,0:T(8,128)(2,1)S(1)} %fusion.new_ref) | copy-start | bytes 1572868
